TPU v7x, 32 devices: a whole 2x2x4 slice. The times are simulated.
32 devices in a mesh: seq: 8 (over z, x), head: 4 (over y, core).
Axes of the slice: x: 2, y: 2, z: 4, core: 2. Of those that a mesh axis runs over, the one named last changes fastest.
Arguments:
- tokens: bfloat16 [4096, 4096], P('seq', 'head'), may hold values from -6 to 6
- norm_gain: float32 [4096], replicated, may hold values from 0.1 to 1.9
- w_query: bfloat16 [4096, 4096], P(None, 'head')
- key_weight: bfloat16 [4096, 1024], P(None, 'head')
- value_weight: bfloat16 [4096, 1024], P(None, 'head'), may hold values from -0.09375 to 0.09375
- w_out: bfloat16 [4096, 4096], P('head'), may hold values from -0.5 to 0.5
- ancestor_blocks: int32 [32, 8], P('seq'), may hold values from -1 to 30, as said below
- visible_counts: int32 [32, 8], P('seq'), may hold values from 0 to 128, as said below
Outputs:
- sublayer_out: bfloat16 [4096, 4096], P('seq', 'head')
Inputs may be any that keep to these rules, and one draw needn't show every extreme that they name: `ancestor_blocks`: entry j of row b is block b's ancestor at depth j (the root block first), an earlier block; entries at and past block b's depth are -1. An ancestor that lies in another index of seq's tokens than block b is always the first block of that index's 512 tokens. The last block's parent is the block before it, whose parent is block 0. `visible_counts`: positive exactly where ancestor_blocks names a block, 0 elsewhere; the last block sees its parent whole.
All inputs are finite; a program needn't handle non-finite values.
Results may differ from a plain program's by a relative error of at most 0.019.
Values may be sent and summed in bfloat16 or wider, within the bound.
A program may use at most 64 MiB of HBM per device.

v0:
```python
import jax
import jax.numpy as jnp
from jax import lax
from jax.sharding import PartitionSpec as P

HEAD_SIZE = 128
BLOCK_TOKENS = 128
DEPTH = 8


ROPE_BASE = 500000.0
NORM_EPS = 1e-05


def rotary_apply(vectors, token_positions):
    midpoint = HEAD_SIZE // 2
    frequency = ROPE_BASE ** (-(jnp.arange(midpoint, dtype=jnp.float32) * 2.0) / HEAD_SIZE)
    angles = token_positions.astype(jnp.float32)[:, None] * frequency[None, :]
    cosine_part = jnp.cos(angles)[:, None, :]
    sine_part = jnp.sin(angles)[:, None, :]
    leading = vectors[..., :midpoint]
    trailing = vectors[..., midpoint:]
    return jnp.concatenate(
        [
            leading * cosine_part - trailing * sine_part,
            trailing * cosine_part + leading * sine_part,
        ],
        axis=-1,
    )


def attend_block(query_rows, own_keys, own_values, near_keys, near_values, seen):
    kv_cols = own_keys.shape[1]
    kv_heads = kv_cols // HEAD_SIZE
    group_size = query_rows.shape[1] // kv_cols
    key_count = (DEPTH + 1) * BLOCK_TOKENS
    all_keys = jnp.concatenate(
        [near_keys.reshape(DEPTH * BLOCK_TOKENS, kv_cols), own_keys], axis=0
    ).reshape(key_count, kv_heads, HEAD_SIZE)
    all_values = jnp.concatenate(
        [near_values.reshape(DEPTH * BLOCK_TOKENS, kv_cols), own_values], axis=0
    ).reshape(key_count, kv_heads, HEAD_SIZE)
    grouped = (
        query_rows.reshape(BLOCK_TOKENS, kv_heads, group_size, HEAD_SIZE)
        .transpose(1, 2, 0, 3)
        .reshape(kv_heads, group_size * BLOCK_TOKENS, HEAD_SIZE)
    )
    scores = jnp.einsum(
        "gqd,kgd->gqk", grouped, all_keys, preferred_element_type=jnp.float32
    ) * HEAD_SIZE ** (-0.5)
    key_index = jnp.arange(key_count, dtype=jnp.int32)
    key_slot = key_index // BLOCK_TOKENS
    key_offset = key_index % BLOCK_TOKENS
    limits = jnp.concatenate([seen, jnp.zeros((1,), jnp.int32)])[key_slot]
    query_offset = jnp.tile(jnp.arange(BLOCK_TOKENS, dtype=jnp.int32), group_size)
    allowed = jnp.where(
        key_slot[None, :] == DEPTH,
        key_offset[None, :] <= query_offset[:, None],
        (key_offset < limits)[None, :],
    )
    masked = jnp.where(allowed[None], scores, -1e30)
    row_max = jnp.max(masked, axis=-1, keepdims=True)
    exponent = jnp.exp(masked - row_max)
    weights = (exponent / jnp.sum(exponent, axis=-1, keepdims=True)).astype(jnp.bfloat16)
    mixed = jnp.einsum(
        "gqk,kgd->gqd", weights, all_values, preferred_element_type=jnp.float32
    ).astype(jnp.bfloat16)
    return (
        mixed.reshape(kv_heads, group_size, BLOCK_TOKENS, HEAD_SIZE)
        .transpose(2, 0, 1, 3)
        .reshape(BLOCK_TOKENS, kv_heads * group_size * HEAD_SIZE)
    )


def local(
    tokens, norm_gain, w_query, key_weight, value_weight, w_out, ancestor_blocks, visible_counts
):
    local_rows = tokens.shape[0]
    blocks_here = local_rows // BLOCK_TOKENS
    gathered = lax.all_gather(tokens, "head", axis=1, tiled=True)
    tok_float = gathered.astype(jnp.float32)
    mean_square = jnp.mean(tok_float * tok_float, axis=1, keepdims=True)
    normed_input = (tok_float * lax.rsqrt(mean_square + NORM_EPS) * norm_gain).astype(jnp.bfloat16)
    queries = jnp.dot(normed_input, w_query, preferred_element_type=jnp.float32)
    key_rows = jnp.dot(normed_input, key_weight, preferred_element_type=jnp.float32)
    value_rows = jnp.dot(normed_input, value_weight, preferred_element_type=jnp.float32)
    base_pos = jnp.sum(visible_counts, axis=1)
    token_positions = jnp.repeat(base_pos, BLOCK_TOKENS) + jnp.tile(
        jnp.arange(BLOCK_TOKENS, dtype=jnp.int32), blocks_here
    )
    query_cols = queries.shape[1]
    kv_cols = key_rows.shape[1]
    queries = (
        rotary_apply(
            queries.reshape(local_rows, query_cols // HEAD_SIZE, HEAD_SIZE), token_positions
        )
        .reshape(local_rows, query_cols)
        .astype(jnp.bfloat16)
    )
    key_rows = (
        rotary_apply(key_rows.reshape(local_rows, kv_cols // HEAD_SIZE, HEAD_SIZE), token_positions)
        .reshape(local_rows, kv_cols)
        .astype(jnp.bfloat16)
    )
    value_rows = value_rows.astype(jnp.bfloat16)
    listed = jnp.clip(ancestor_blocks, 0, None)
    all_keys, all_values = (
        lax.all_gather(key_rows, "seq", axis=0, tiled=True),
        lax.all_gather(value_rows, "seq", axis=0, tiled=True),
    )
    blocked_keys = all_keys.reshape(-1, BLOCK_TOKENS, kv_cols)
    blocked_values = all_values.reshape(-1, BLOCK_TOKENS, kv_cols)
    near_keys = blocked_keys[listed]
    near_values = blocked_values[listed]

    def one_block(inputs):
        query_rows, own_keys, own_values, block_keys, block_values, seen = inputs
        return attend_block(query_rows, own_keys, own_values, block_keys, block_values, seen)

    attention = lax.map(
        one_block,
        (
            queries.reshape(blocks_here, BLOCK_TOKENS, query_cols),
            key_rows.reshape(blocks_here, BLOCK_TOKENS, kv_cols),
            value_rows.reshape(blocks_here, BLOCK_TOKENS, kv_cols),
            near_keys,
            near_values,
            visible_counts,
        ),
    )
    attention = attention.reshape(local_rows, query_cols)
    partial_term = jnp.dot(attention, w_out, preferred_element_type=jnp.float32)
    summed = lax.psum_scatter(
        partial_term.astype(jnp.bfloat16), "head", scatter_dimension=1, tiled=True
    )
    return summed


def solution(mesh):
    placed = (
        P("seq", "head"),
        P(),
        P(None, "head"),
        P(None, "head"),
        P(None, "head"),
        P("head", None),
        P("seq", None),
        P("seq", None),
    )
    return jax.shard_map(
        local, mesh=mesh, in_specs=placed, out_specs=P("seq", "head"), check_vma=False
    )
```

profile of v0, /device:TPU:0, one launch (start us, length us, event | category | flops | bytes accessed | tf_op | source)
XLA Modules:
  0.0 303.0 jit_solution(13206481070883029090)
XLA Ops:
  7.3 38.8 %all-gather.4.cloned.1.call-done = bf16[512,4096]{1,0:T(8,128)(2,1)} async-done(((bf16[512,1024]{1,0:T(8,128)(2,1)}), bf16[512,4096]{1,0:T(8,128)(2,1)}) %all-gather.4.cloned.1.call-update) | async-done | bytes 4194320 | tf_op jit(solution)/shard_map/all_gather | solution.py:80
  46.1 3.2 %fusion.42 = f32[512]{0:T(512)S(1)} fusion(bf16[512,4096]{1,0:T(8,128)(2,1)} %all-gather.4.cloned.1.call-done), kind=kLoop, calls=%fused_computation.63 | loop fusion | flops 6290944 | bytes 4196352 | tf_op jit(solution)/shard_map/reduce_sum | solution.py:82
  49.6 2.0 convolution_convert_fusion.1
  51.9 1.0 multiply_cosine_fusion
  52.9 4.4 %fusion.46 = f32[512,256]{0,1:T(8,128)S(1)} fusion(bf16[4096,256]{1,0:T(8,128)(2,1)} %param.13, bf16[512,4096]{1,0:T(8,128)(2,1)} %all-gather.4.cloned.1.call-done, f32[4096]{0:T(1024)S(1)} %copy-done.5, f32[512]{0:T(512)S(1)} %add_rsqrt_fusion), kind=kOutput, calls=%fused_computation.83 | convolution fusion | flops 1082130432 | bytes 6834176 | tf_op jit(solution)/shard_map/dot_general | solution.py:85
  57.3 0.7 fusion.52
  58.1 1.2 copy.43
  59.3 1.0 copy.42
  60.3 1.6 multiply_subtract_fusion
  62.6 0.7 copy.51
  63.7 0.9 convert_element_type.57
  64.6 8.3 %convolution_bitcast_fusion = f32[64,8,8,128]{3,1,2,0:T(8,128)S(1)} fusion(bf16[4096,1024]{1,0:T(8,128)(2,1)} %param.12, bf16[512,4096]{1,0:T(8,128)(2,1)} %all-gather.4.cloned.1.call-done, f32[4096]{0:T(1024)S(1)} %copy-done.5, f32[512]{0:T(512)S(1)} %add_rsqrt_fusion), kind=kOutput, calls=%fused_computation.69 | convolution fusion | flops 4303355904 | bytes 14698496 | tf_op jit(solution)/shard_map/dot_general | solution.py:84
  73.4 0.9 subtract_convert_fusion
  74.8 1.3 convert_element_type.54
  76.2 24.9 %all-gather.8.cloned.1.call-done = bf16[4096,256]{1,0:T(8,128)(2,1)} async-done(((bf16[512,256]{1,0:T(8,128)(2,1)}), bf16[4096,256]{1,0:T(8,128)(2,1)}) %all-gather.8.cloned.1.call-update) | async-done | bytes 2097168 | tf_op jit(solution)/shard_map/all_gather | solution.py:109
  101.1 3.6 %gather_fusion.1 = bf16[32,128,256]{2,1,0:T(8,128)(2,1)} fusion(bf16[32,128,256]{2,1,0:T(8,128)(2,1)} %bitcast.88, s32[1024]{0:T(1024)S(1)} %pad_clamp_fusion), kind=kCustom, calls=%fused_computation.1 | custom fusion | bytes 4194432 | tf_op jit(solution)/shard_map/gather | solution.py:114
  104.7 46.3 %all-gather.6.cloned.1.call-done = bf16[4096,256]{1,0:T(8,128)(2,1)} async-done(((bf16[512,256]{1,0:T(8,128)(2,1)}), bf16[4096,256]{1,0:T(8,128)(2,1)}) %all-gather.6.cloned.1.call-update) | async-done | bytes 2097168 | tf_op jit(solution)/shard_map/all_gather | solution.py:108
  151.0 3.6 %gather_fusion = bf16[32,128,256]{2,1,0:T(8,128)(2,1)} fusion(bf16[32,128,256]{2,1,0:T(8,128)(2,1)} %bitcast.89, s32[1024]{0:T(1024)S(1)} %pad_clamp_fusion), kind=kCustom, calls=%fused_computation | custom fusion | bytes 4194432 | tf_op jit(solution)/shard_map/gather | solution.py:113
  154.6 88.5 %while.12 = (s32[]{:T(128)}, bf16[4,128,1024]{2,1,0:T(8,128)(2,1)}, s32[4,8]{1,0:T(4,128)S(1)}, bf16[4,128,1024]{2,1,0:T(8,128)(2,1)}, bf16[4,8,128,256]{3,2,1,0...) while((s32[]{:T(128)}, bf16[4,128,1024]{2,1,0:T(8,128)(2,1)}, ...), condition=%wide.region_5.6_spmd, body=%wide.region_2.5_spmd.sunk | while | flops 921518976 | bytes 16686389 | solution.py:120
  155.3 4.3 %fusion.77 = s32[1152]{0:T(1024)S(1)} fusion(s32[]{:T(128)} %bitcast.67, s32[]{:T(128)} %bitcast.68, s32[]{:T(128)} %bitcast.69, s32[]{:T(128)} %bitcast.70, s32[]{:T(128)} %bitcast.71, s32[]{:T(128)} %bitcast.72, s32[]{:T(128)} %bitcast.73), kind=kLoop, calls=%fused_computation.43.clone.1 | loop fusion | flops 26496 | bytes 4636 | tf_op jit(solution)/shard_map/while/body/eval_jaxpr/gather | solution.py:54
  160.3 0.9 constant_dynamic-slice_fusion.12
  161.6 1.0 constant_dynamic-slice_fusion.10
  163.0 1.3 compare_select_fusion.9
  164.3 1.3 constant_dynamic-slice_fusion.13
  165.6 0.9 reshape.387
  166.5 1.1 copy.65
  167.6 0.8 copy-done.1
  168.4 3.0 exponential_reduce_fusion.2
  171.6 3.9 %fusion.79 = bf16[2,512,128]{2,1,0:T(8,128)(2,1)S(1)} fusion(f32[2,512]{1,0:T(2,128)S(1)} %exponential_reduce_fusion.2, bf16[128,2,128]{2,0,1:T(8,128)(2,1)S(1)} %copy.67, bf16[1024,2,128]{2,0,1:T(8,128)(2,1)S(1)} %copy.68, bf16[2,512,128]{2,1,0:T(8,128)(2,1)S(1)} %bitcast.83, pred[512,1152]{1,0:T(8,128)(4,1)} %compare_select_fusion.9, ...), kind=kOutput, calls=%fused_computation.10.clone.1 | convolution fusion | flops 612370560 | bytes 2297856 | tf_op jit(solution)/shard_map/while/body/eval_jaxpr/gqk,kgd->gqd/dot_general | solution.py:65
  176.0 0.7 constant_dynamic-update-slice_fusion.2
  177.5 4.3 %fusion.77 = s32[1152]{0:T(1024)S(1)} fusion(s32[]{:T(128)} %bitcast.67, s32[]{:T(128)} %bitcast.68, s32[]{:T(128)} %bitcast.69, s32[]{:T(128)} %bitcast.70, s32[]{:T(128)} %bitcast.71, s32[]{:T(128)} %bitcast.72, s32[]{:T(128)} %bitcast.73), kind=kLoop, calls=%fused_computation.43.clone.1 | loop fusion | flops 26496 | bytes 4636 | tf_op jit(solution)/shard_map/while/body/eval_jaxpr/gather | solution.py:54
  182.4 0.9 constant_dynamic-slice_fusion.12
  183.8 1.0 constant_dynamic-slice_fusion.10
  185.1 1.3 compare_select_fusion.9
  186.4 1.3 constant_dynamic-slice_fusion.13
  187.7 0.9 reshape.387
  188.6 1.1 copy.65
  189.8 0.8 copy-done.1
  190.6 3.0 exponential_reduce_fusion.2
  193.8 3.9 %fusion.79 = bf16[2,512,128]{2,1,0:T(8,128)(2,1)S(1)} fusion(f32[2,512]{1,0:T(2,128)S(1)} %exponential_reduce_fusion.2, bf16[128,2,128]{2,0,1:T(8,128)(2,1)S(1)} %copy.67, bf16[1024,2,128]{2,0,1:T(8,128)(2,1)S(1)} %copy.68, bf16[2,512,128]{2,1,0:T(8,128)(2,1)S(1)} %bitcast.83, pred[512,1152]{1,0:T(8,128)(4,1)} %compare_select_fusion.9, ...), kind=kOutput, calls=%fused_computation.10.clone.1 | convolution fusion | flops 612370560 | bytes 2297856 | tf_op jit(solution)/shard_map/while/body/eval_jaxpr/gqk,kgd->gqd/dot_general | solution.py:65
  198.1 0.7 constant_dynamic-update-slice_fusion.2
  199.6 4.3 %fusion.77 = s32[1152]{0:T(1024)S(1)} fusion(s32[]{:T(128)} %bitcast.67, s32[]{:T(128)} %bitcast.68, s32[]{:T(128)} %bitcast.69, s32[]{:T(128)} %bitcast.70, s32[]{:T(128)} %bitcast.71, s32[]{:T(128)} %bitcast.72, s32[]{:T(128)} %bitcast.73), kind=kLoop, calls=%fused_computation.43.clone.1 | loop fusion | flops 26496 | bytes 4636 | tf_op jit(solution)/shard_map/while/body/eval_jaxpr/gather | solution.py:54
  204.5 0.9 constant_dynamic-slice_fusion.12
  205.9 1.0 constant_dynamic-slice_fusion.10
  207.2 1.3 compare_select_fusion.9
  208.5 1.3 constant_dynamic-slice_fusion.13
  209.8 0.9 reshape.387
  210.7 1.1 copy.65
  211.9 0.8 copy-done.1
  212.7 3.0 exponential_reduce_fusion.2
  215.9 3.9 %fusion.79 = bf16[2,512,128]{2,1,0:T(8,128)(2,1)S(1)} fusion(f32[2,512]{1,0:T(2,128)S(1)} %exponential_reduce_fusion.2, bf16[128,2,128]{2,0,1:T(8,128)(2,1)S(1)} %copy.67, bf16[1024,2,128]{2,0,1:T(8,128)(2,1)S(1)} %copy.68, bf16[2,512,128]{2,1,0:T(8,128)(2,1)S(1)} %bitcast.83, pred[512,1152]{1,0:T(8,128)(4,1)} %compare_select_fusion.9, ...), kind=kOutput, calls=%fused_computation.10.clone.1 | convolution fusion | flops 612370560 | bytes 2297856 | tf_op jit(solution)/shard_map/while/body/eval_jaxpr/gqk,kgd->gqd/dot_general | solution.py:65
  220.2 0.7 constant_dynamic-update-slice_fusion.2
  221.7 4.3 %fusion.77 = s32[1152]{0:T(1024)S(1)} fusion(s32[]{:T(128)} %bitcast.67, s32[]{:T(128)} %bitcast.68, s32[]{:T(128)} %bitcast.69, s32[]{:T(128)} %bitcast.70, s32[]{:T(128)} %bitcast.71, s32[]{:T(128)} %bitcast.72, s32[]{:T(128)} %bitcast.73), kind=kLoop, calls=%fused_computation.43.clone.1 | loop fusion | flops 26496 | bytes 4636 | tf_op jit(solution)/shard_map/while/body/eval_jaxpr/gather | solution.py:54
  226.6 0.9 constant_dynamic-slice_fusion.12
  228.0 1.0 constant_dynamic-slice_fusion.10
  229.3 1.3 compare_select_fusion.9
  230.7 1.3 constant_dynamic-slice_fusion.13
  231.9 0.9 reshape.387
  232.9 1.1 copy.65
  234.0 0.8 copy-done.1
  234.8 3.0 exponential_reduce_fusion.2
  238.0 3.9 %fusion.79 = bf16[2,512,128]{2,1,0:T(8,128)(2,1)S(1)} fusion(f32[2,512]{1,0:T(2,128)S(1)} %exponential_reduce_fusion.2, bf16[128,2,128]{2,0,1:T(8,128)(2,1)S(1)} %copy.67, bf16[1024,2,128]{2,0,1:T(8,128)(2,1)S(1)} %copy.68, bf16[2,512,128]{2,1,0:T(8,128)(2,1)S(1)} %bitcast.83, pred[512,1152]{1,0:T(8,128)(4,1)} %compare_select_fusion.9, ...), kind=kOutput, calls=%fused_computation.10.clone.1 | convolution fusion | flops 612370560 | bytes 2297856 | tf_op jit(solution)/shard_map/while/body/eval_jaxpr/gqk,kgd->gqd/dot_general | solution.py:65
  243.1 10.2 %convolution_convert_fusion = bf16[512,4096]{1,0:T(8,128)(2,1)} fusion(bf16[512,1024]{1,0:T(8,128)(2,1)} %bitcast.92, bf16[1024,4096]{1,0:T(8,128)(2,1)} %param.15), kind=kOutput, calls=%fused_computation.66 | convolution fusion | flops 4297064448 | bytes 13631488 | tf_op jit(solution)/shard_map/dot_general | solution.py:132
  253.3 43.2 %reduce-scatter.2.cloned.1.call-done = bf16[512,1024]{1,0:T(8,128)(2,1)} async-done(((bf16[512,4096]{1,0:T(8,128)(2,1)}), bf16[512,1024]{1,0:T(8,128)(2,1)}) %reduce-scatter.2.cloned.1.call-update) | async-done | bytes 1048592 | tf_op jit(solution)/shard_map/reduce_scatter | solution.py:133
  (102 shorter events, 15.0 us)
Async XLA Ops:
  6.5 42.8 %copy-start = (bf16[4096,256]{1,0:T(8,128)(2,1)S(1)}, bf16[4096,256]{1,0:T(8,128)(2,1)}, u32[]{:S(2)}) copy-start(bf16[4096,256]{1,0:T(8,128)(2,1)} %param.14) | copy-start | bytes 6291460
  6.5 42.9 %copy-start.5 = (f32[4096]{0:T(1024)S(1)}, f32[4096]{0:T(1024)}, u32[]{:S(2)}) copy-start(f32[4096]{0:T(1024)} %param.11) | copy-start | bytes 49156
  6.5 39.6 %all-gather.4.cloned.1.call-start = ((), (), s32[]{:S(2)}) async-start(), calls=%async_computation.1 | async-start | bytes 5242880 | tf_op jit(solution)/shard_map/all_gather | solution.py:80
  7.3 93.8 %all-gather.8.cloned.1.call-start = ((), (), s32[]{:S(2)}) async-start(), calls=%async_computation.3 | async-start | bytes 2359296 | tf_op jit(solution)/shard_map/all_gather | solution.py:109
  46.1 3.4 %copy-start.2 = (bf16[512,4096]{1,0:T(8,128)(2,1)S(1)}, bf16[512,4096]{1,0:T(8,128)(2,1)}, u32[]{:S(2)}) copy-start(bf16[512,4096]{1,0:T(8,128)(2,1)} %all-gather.4.cloned.1.call-done) | copy-start | bytes 12582916
  49.6 2.1 copy-start.3
  51.6 99.4 %all-gather.6.cloned.1.call-start = ((), (), s32[]{:S(2)}) async-start(), calls=%async_computation.2 | async-start | bytes 2359296 | tf_op jit(solution)/shard_map/all_gather | solution.py:108
  57.3 6.3 %copy-start.4 = (s32[4,8]{1,0:T(4,128)S(1)}, s32[4,8]{1,0:T(4,128)}, u32[]{:S(2)}) copy-start(s32[4,8]{1,0:T(4,128)} %param.16) | copy-start | bytes 388
  63.4 233.1 %reduce-scatter.2.cloned.1.call-start = ((), (), s32[]{:S(2)}) async-start(), calls=%async_computation.4 | async-start | bytes 5242880 | tf_op jit(solution)/shard_map/reduce_scatter | solution.py:133
  167.6 0.8 copy-start.1
  189.7 0.8 copy-start.1
  211.9 0.8 copy-start.1
  234.0 0.8 copy-start.1
Sparse Core Ops, SparseCore 0:
  8.9 37.1 all-gather.3
  51.8 49.2 all-gather.7
  103.2 47.7 all-gather.5
  253.4 43.0 reduce-scatter.1
where the time goes:
time: 304 us; the launch traced here: 303 us
  waiting for transfers between devices  154 us (51%)
  matrix products  52.6 us (17%)
  local copies, waits for them, and re-layouts  49 us (16%)
  other arithmetic  33.3 us (11%)
  between operations  13.2 us (4%)
    all_gather x1, waiting for transfers between devices, local(): lax.all_gather(key_rows, 'seq', axis=0, tiled=True)  46.3 us
    reduce_scatter x1, waiting for transfers between devices, local(): lax.psum_scatter(partial_term.astype(jnp.bfloat16), 'head', scatter_dimen...  43.2 us
    all_gather x1, waiting for transfers between devices, local(): gathered = lax.all_gather(tokens, 'head', axis=1, tiled=True)  38.8 us
    all_gather x1, waiting for transfers between devices, local(): lax.all_gather(value_rows, 'seq', axis=0, tiled=True)  24.9 us
    gather x12, other arithmetic, attend_block(): limits = jnp.concatenate([seen, jnp.zeros((1,), jnp.int32)])[key_slot]  17.5 us
    dot_general x4, matrix products, attend_block(): jnp.einsum('gqk,kgd->gqd', weights, all_values, preferred_element_type=jn...  15.8 us
    dynamic_slice x28, local copies, waits for them, and re-layouts, local(): lax.map(one_block, (queries.reshape(blocks_here, BLOCK_TOKENS, query_cols...  14.1 us
    sub x4, matrix products, attend_block(): exponent = jnp.exp(masked - row_max)  12 us
  transfers between devices with their start and end apart: 4, of which 4 were waited for; matrix products, arithmetic and copies ran while one was open for 9% of the time, Pallas kernels for 0%

commit v1 on v0

v1 whole, which is shorter than its diff:
```python
import functools

import numpy as np

import jax
import jax.numpy as jnp
from jax import lax
from jax.experimental import pallas as pl
from jax.experimental.pallas import tpu as pltpu
from jax.sharding import PartitionSpec as P

HEAD_SIZE = 128
BLOCK_TOKENS = 128
DEPTH = 8
ROPE_BASE = 500000.0
NORM_EPS = 1e-05
MESH = pl.DeviceIdType.MESH
SLOTS = DEPTH + 1
KEYS = SLOTS * BLOCK_TOKENS
LOG2E = 1.4426950408889634


def kernel(
    n_seq,
    n_head,
    tok_ref,
    gain_ref,
    freq_ref,
    wq_ref,
    wk_ref,
    wv_ref,
    wo_ref,
    anc_ref,
    vis_ref,
    out_ref,
    xbuf,
    wq,
    wk,
    wv,
    wo,
    normed,
    qbuf,
    kvbuf,
    kvcat,
    bias,
    attn,
    psend,
    precv,
    osum,
    acc,
    ysend,
    yrecv,
    w_sem,
    own_sem,
    ty_send,
    ty_recv,
    tc_send,
    tc_recv,
    tf_send,
    tf_recv,
    kz_send,
    kz_recv,
    kx_send,
    kx_recv,
    p_send,
    p_recv,
    r_send,
    r_recv,
):
    rows, width = tok_ref.shape
    blocks = rows // BLOCK_TOKENS
    q_cols = wq.shape[1]
    kv_cols = wk.shape[1]
    kv_heads = kv_cols // HEAD_SIZE
    group = q_cols // kv_cols
    ny = n_head // 2
    nx = ny
    nz = n_seq // nx
    seq = lax.axis_index("seq")
    head = lax.axis_index("head")
    y, core = lax.div(head, 2), lax.rem(head, 2)
    z, x = lax.div(seq, nx), lax.rem(seq, nx)
    partner = 2 * y + 1 - core

    def y_peer(j):
        return 2 * lax.rem(y + j, ny) + core

    def z_peer(j):
        return lax.rem(z + j, nz) * nx + x

    def x_peer(i):
        return z * nx + lax.rem(x + i, nx)

    def remote(src, dst, send, recv, seq_id, head_id):
        return pltpu.make_async_remote_copy(
            src_ref=src,
            dst_ref=dst,
            send_sem=send,
            recv_sem=recv,
            device_id=(seq_id, head_id),
            device_id_type=MESH,
        )

    barrier = pltpu.get_barrier_semaphore()
    peers = [(seq, partner)]
    peers += [(seq, y_peer(j)) for j in range(1, ny)]
    peers += [(z_peer(j), head) for j in range(1, nz)]
    peers += [(x_peer(i), head) for i in range(1, nx)]
    for peer in peers:
        pl.semaphore_signal(barrier, inc=1, device_id=peer, device_id_type=MESH)

    def weight_copy(i):
        source = (wk_ref, wv_ref, wq_ref, wo_ref)[i]
        return pltpu.make_async_copy(source, (wk, wv, wq, wo)[i], w_sem.at[i])

    def token_rows(b):
        return tok_ref.at[pl.ds(pl.multiple_of(b * BLOCK_TOKENS, BLOCK_TOKENS), BLOCK_TOKENS)]

    def own_copy(b):
        return pltpu.make_async_copy(token_rows(b), xbuf.at[b, head], own_sem.at[b])

    def tok_y(b, j):
        return remote(
            token_rows(b), xbuf.at[b, head], ty_send.at[b, j - 1], ty_recv.at[b, j - 1], seq, y_peer(j)
        )

    def tok_y_in(b, j):
        slot = xbuf.at[b, y_peer(ny - j)]
        return remote(slot, slot, ty_send.at[b, j - 1], ty_recv.at[b, j - 1], seq, y_peer(ny - j))

    def tok_core(b):
        return remote(token_rows(b), xbuf.at[b, head], tc_send.at[b], tc_recv.at[b], seq, partner)

    def tok_core_in(b):
        slot = xbuf.at[b, partner]
        return remote(slot, slot, tc_send.at[b], tc_recv.at[b], seq, partner)

    def tok_fwd(b, j):
        slot = xbuf.at[b, y_peer(ny - j)]
        return remote(slot, slot, tf_send.at[b, j - 1], tf_recv.at[b, j - 1], seq, partner)

    def tok_fwd_in(b, j):
        slot = xbuf.at[b, 2 * lax.rem(y + ny - j, ny) + 1 - core]
        return remote(slot, slot, tf_send.at[b, j - 1], tf_recv.at[b, j - 1], seq, partner)

    def kv_z(j):
        return remote(
            kvbuf.at[n_seq], kvbuf.at[seq], kz_send.at[j - 1], kz_recv.at[j - 1], z_peer(j), head
        )

    def kv_z_in(j):
        slot = kvbuf.at[z_peer(nz - j)]
        return remote(slot, slot, kz_send.at[j - 1], kz_recv.at[j - 1], z_peer(nz - j), head)

    def kv_x(j, i):
        src = kvbuf.at[n_seq] if j == 0 else kvbuf.at[z_peer(nz - j)]
        dst = kvbuf.at[seq] if j == 0 else kvbuf.at[z_peer(nz - j)]
        return remote(src, dst, kx_send.at[j, i - 1], kx_recv.at[j, i - 1], x_peer(i), head)

    def kv_x_in(j, i):
        slot = kvbuf.at[lax.rem(z + nz - j, nz) * nx + lax.rem(x + nx - i, nx)]
        return remote(slot, slot, kx_send.at[j, i - 1], kx_recv.at[j, i - 1], x_peer(nx - i), head)

    def part_core(b):
        return remote(psend.at[b], precv.at[b], p_send.at[b], p_recv.at[b], seq, partner)

    def part_y(b, j):
        return remote(
            ysend.at[b, j - 1],
            yrecv.at[b, j - 1],
            r_send.at[b, j - 1],
            r_recv.at[b, j - 1],
            seq,
            y_peer(j),
        )

    for b in range(blocks):
        own_copy(b).start()
    for i in range(4):
        weight_copy(i).start()
    pl.semaphore_wait(barrier, len(peers))
    for b in range(blocks):
        for j in range(1, ny):
            tok_y(b, j).start()
        tok_core(b).start()

    def project(b, carry):
        for j in range(1, ny):
            tok_y_in(b, j).wait_recv()
            tok_fwd(b, j).start()
        own_copy(b).wait()
        tok_core_in(b).wait_recv()

        @pl.when(b == 2)
        def _():
            for j in range(1, nz):
                kv_z_in(j).wait_recv()
                for i in range(1, nx):
                    kv_x(j, i).start()

        for j in range(1, ny):
            tok_fwd_in(b, j).wait_recv()

        square = jnp.zeros((BLOCK_TOKENS, 1), jnp.float32)
        for k in range(n_head):
            piece = xbuf[b, k].astype(jnp.float32)
            square += jnp.sum(piece * piece, axis=1, keepdims=True)
        scale = lax.rsqrt(square / (n_head * width) + NORM_EPS)
        for k in range(n_head):
            piece = xbuf[b, k].astype(jnp.float32)
            cols = slice(k * width, (k + 1) * width)
            normed[:, cols] = (piece * scale * gain_ref[:, cols]).astype(jnp.bfloat16)

        base = vis_ref[b, 0]
        for j in range(1, DEPTH):
            base += vis_ref[b, j]
        position = base + lax.broadcasted_iota(jnp.int32, (BLOCK_TOKENS, HEAD_SIZE), 0)
        angle = position.astype(jnp.float32) * freq_ref[...]
        lane = lax.broadcasted_iota(jnp.int32, (BLOCK_TOKENS, HEAD_SIZE), 1)
        cosine = jnp.cos(angle)
        sine = jnp.sin(angle)
        sine = jnp.where(lane < HEAD_SIZE // 2, -sine, sine)

        def rope(vectors):
            return vectors * cosine + pltpu.roll(vectors, HEAD_SIZE // 2, 1) * sine

        @pl.when(b == 0)
        def _():
            weight_copy(0).wait()
            weight_copy(1).wait()

        keys = jnp.dot(normed[...], wk[...], preferred_element_type=jnp.float32)
        for g in range(kv_heads):
            cols = slice(g * HEAD_SIZE, (g + 1) * HEAD_SIZE)
            kvbuf[n_seq + b, :, cols] = rope(keys[:, cols]).astype(jnp.bfloat16)
        values = jnp.dot(normed[...], wv[...], preferred_element_type=jnp.float32)
        kvbuf[n_seq + b, :, kv_cols:] = values.astype(jnp.bfloat16)

        @pl.when(b == 0)
        def _():
            for j in range(1, nz):
                kv_z(j).start()
            for i in range(1, nx):
                kv_x(0, i).start()
            weight_copy(2).wait()

        tile = 2 * HEAD_SIZE

        def query_tile(t, inner):
            cols = pl.ds(pl.multiple_of(t * tile, tile), tile)
            found = jnp.dot(normed[...], wq[:, cols], preferred_element_type=jnp.float32)
            for k in range(2):
                turned = rope(found[:, k * HEAD_SIZE : (k + 1) * HEAD_SIZE])
                qbuf[b, 2 * t + k] = (turned * (HEAD_SIZE**-0.5 * LOG2E)).astype(jnp.bfloat16)
            return inner

        lax.fori_loop(0, q_cols // tile, query_tile, 0)
        return carry

    lax.fori_loop(0, blocks, project, 0)

    weight_copy(3).wait()
    for j in range(nz):
        for i in range(1, nx):
            kv_x_in(j, i).wait_recv()

    def attend(b, carry):
        lane = lax.broadcasted_iota(jnp.int32, (BLOCK_TOKENS, BLOCK_TOKENS), 1)
        row = lax.broadcasted_iota(jnp.int32, (BLOCK_TOKENS, BLOCK_TOKENS), 0)
        for j in range(SLOTS):
            part = slice(j * BLOCK_TOKENS, (j + 1) * BLOCK_TOKENS)
            if j < DEPTH:
                block_id = jnp.maximum(anc_ref[b, j], 0)
                owner, inside = lax.div(block_id, blocks), lax.rem(block_id, blocks)
                slot = jnp.where(owner == seq, n_seq + inside, owner)
                allowed = lane < vis_ref[b, j]
            else:
                slot = n_seq + b
                allowed = lane <= row
            kvcat[part] = kvbuf[slot]
            bias[:, part] = jnp.where(allowed, 0.0, -1e30)

        for g in range(kv_heads):
            query = qbuf[b, g * group : (g + 1) * group].reshape(
                group * BLOCK_TOKENS, HEAD_SIZE
            )
            key = kvcat[:, g * HEAD_SIZE : (g + 1) * HEAD_SIZE]
            value = kvcat[:, kv_cols + g * HEAD_SIZE : kv_cols + (g + 1) * HEAD_SIZE]
            scores = lax.dot_general(
                query, key, (((1,), (1,)), ((), ())), preferred_element_type=jnp.float32
            )
            scores = (
                scores.reshape(group, BLOCK_TOKENS, KEYS) + bias[...][None]
            ).reshape(group * BLOCK_TOKENS, KEYS)
            top = jnp.max(scores, axis=1, keepdims=True)
            weight = jnp.exp2(scores - top)
            total = jnp.sum(weight, axis=1, keepdims=True)
            mixed = jnp.dot(
                weight.astype(jnp.bfloat16), value, preferred_element_type=jnp.float32
            )
            mixed = (mixed / total).astype(jnp.bfloat16)
            for k in range(group):
                at = (g * group + k) * HEAD_SIZE
                attn[:, at : at + HEAD_SIZE] = mixed[k * BLOCK_TOKENS : (k + 1) * BLOCK_TOKENS]

        tile = 512
        per = width // tile

        def other_tile(t, inner):
            k, m = lax.div(t, per), lax.rem(t, per)
            cols = pl.ds(pl.multiple_of((2 * k + 1 - core) * width + m * tile, tile), tile)
            into = pl.ds(pl.multiple_of(m * tile, tile), tile)
            found = jnp.dot(attn[...], wo[:, cols], preferred_element_type=jnp.float32)
            psend[b, k, :, into] = found.astype(jnp.bfloat16)
            return inner

        lax.fori_loop(0, ny * per, other_tile, 0)
        part_core(b).start()

        def own_tile(t, inner):
            k, m = lax.div(t, per), lax.rem(t, per)
            cols = pl.ds(pl.multiple_of((2 * k + core) * width + m * tile, tile), tile)
            into = pl.ds(pl.multiple_of(m * tile, tile), tile)
            osum[k, :, into] = jnp.dot(attn[...], wo[:, cols], preferred_element_type=jnp.float32)
            return inner

        lax.fori_loop(0, ny * per, own_tile, 0)
        part_core(b).wait_recv()
        for j in range(1, ny):
            k = lax.rem(y + j, ny)
            ysend[b, j - 1] = (osum[k] + precv[b, k].astype(jnp.float32)).astype(jnp.bfloat16)
            part_y(b, j).start()
        acc[b] = osum[y] + precv[b, y].astype(jnp.float32)
        return carry

    lax.fori_loop(0, blocks, attend, 0)

    def finish(b, carry):
        result = acc[b]
        for j in range(1, ny):
            part_y(b, j).wait_recv()
            result += yrecv[b, j - 1].astype(jnp.float32)
        out_ref[pl.ds(pl.multiple_of(b * BLOCK_TOKENS, BLOCK_TOKENS), BLOCK_TOKENS)] = (
            result.astype(jnp.bfloat16)
        )
        for j in range(1, ny):
            tok_y(b, j).wait_send()
            tok_fwd(b, j).wait_send()
            part_y(b, j).wait_send()
        tok_core(b).wait_send()
        part_core(b).wait_send()
        return carry

    lax.fori_loop(0, blocks, finish, 0)
    for j in range(1, nz):
        kv_z(j).wait_send()
    for j in range(nz):
        for i in range(1, nx):
            kv_x(j, i).wait_send()


def local(
    n_seq,
    n_head,
    tokens,
    norm_gain,
    w_query,
    key_weight,
    value_weight,
    w_out,
    ancestor_blocks,
    visible_counts,
):
    rows, width = tokens.shape
    blocks = rows // BLOCK_TOKENS
    q_cols = w_query.shape[1]
    kv_cols = key_weight.shape[1]
    ny = n_head // 2
    nx = ny
    nz = n_seq // nx
    half = HEAD_SIZE // 2
    frequency = ROPE_BASE ** (-(np.arange(half) * 2.0) / HEAD_SIZE)
    frequency = np.concatenate([frequency, frequency]).astype(np.float32)[None]
    dma = pltpu.SemaphoreType.DMA
    vmem = pl.BlockSpec(memory_space=pltpu.VMEM)
    smem = pl.BlockSpec(memory_space=pltpu.SMEM)
    hbm = pl.BlockSpec(memory_space=pl.ANY)
    bf16, f32 = jnp.bfloat16, jnp.float32
    return pl.pallas_call(
        functools.partial(kernel, n_seq, n_head),
        out_shape=jax.ShapeDtypeStruct((rows, width), bf16),
        in_specs=[hbm, vmem, vmem, hbm, hbm, hbm, hbm, smem, smem],
        out_specs=vmem,
        scratch_shapes=[
            pltpu.VMEM((blocks, n_head, BLOCK_TOKENS, width), bf16),
            pltpu.VMEM(w_query.shape, bf16),
            pltpu.VMEM(key_weight.shape, bf16),
            pltpu.VMEM(value_weight.shape, bf16),
            pltpu.VMEM(w_out.shape, bf16),
            pltpu.VMEM((BLOCK_TOKENS, n_head * width), bf16),
            pltpu.VMEM((blocks, q_cols // HEAD_SIZE, BLOCK_TOKENS, HEAD_SIZE), bf16),
            pltpu.VMEM((n_seq + blocks, BLOCK_TOKENS, 2 * kv_cols), bf16),
            pltpu.VMEM((KEYS, 2 * kv_cols), bf16),
            pltpu.VMEM((BLOCK_TOKENS, KEYS), f32),
            pltpu.VMEM((BLOCK_TOKENS, q_cols), bf16),
            pltpu.VMEM((blocks, ny, BLOCK_TOKENS, width), bf16),
            pltpu.VMEM((blocks, ny, BLOCK_TOKENS, width), bf16),
            pltpu.VMEM((ny, BLOCK_TOKENS, width), f32),
            pltpu.VMEM((blocks, BLOCK_TOKENS, width), f32),
            pltpu.VMEM((blocks, ny - 1, BLOCK_TOKENS, width), bf16),
            pltpu.VMEM((blocks, ny - 1, BLOCK_TOKENS, width), bf16),
            dma((4,)),
            dma((blocks,)),
            dma((blocks, ny - 1)),
            dma((blocks, ny - 1)),
            dma((blocks,)),
            dma((blocks,)),
            dma((blocks, ny - 1)),
            dma((blocks, ny - 1)),
            dma((nz - 1,)),
            dma((nz - 1,)),
            dma((nz, nx - 1)),
            dma((nz, nx - 1)),
            dma((blocks,)),
            dma((blocks,)),
            dma((blocks, ny - 1)),
            dma((blocks, ny - 1)),
        ],
        compiler_params=pltpu.CompilerParams(
            collective_id=0, has_side_effects=True, vmem_limit_bytes=60 * 1024 * 1024
        ),
        cost_estimate=pl.CostEstimate(
            flops=13 * 10**9, bytes_accessed=25 * 10**6, transcendentals=5 * 10**6
        ),
    )(
        tokens,
        norm_gain[None],
        jnp.asarray(frequency),
        w_query,
        key_weight,
        value_weight,
        w_out,
        ancestor_blocks,
        visible_counts,
    )


def solution(mesh):
    placed = (
        P("seq", "head"),
        P(),
        P(None, "head"),
        P(None, "head"),
        P(None, "head"),
        P("head", None),
        P("seq", None),
        P("seq", None),
    )
    return jax.shard_map(
        functools.partial(local, mesh.shape["seq"], mesh.shape["head"]),
        mesh=mesh,
        in_specs=placed,
        out_specs=P("seq", "head"),
        check_vma=False,
    )
```

time: 304 us -> 70.6 us (0.23)
  waiting for transfers between devices: 154 us -> 0 us
  Pallas kernels: 0 us -> 68.1 us
  matrix products: 52.6 us -> 0 us
  local copies, waits for them, and re-layouts: 49 us -> 2.26 us
  other arithmetic: 33.3 us -> 0 us
  between operations: 13.2 us -> 0.01 us
    all_gather x3 -> x0, waiting for transfers between devices: 110 us -> none  [the longest x1 46.3 us: local(): lax.all_gather(key_rows, 'seq', axis=0, tiled=True)]
    pallas_call x0 -> x1, Pallas kernels: none -> 68.1 us  [local(): pl.pallas_call(functools.partial(kernel, n_seq, n_head), out_shape=jax.Sh...]
    reduce_scatter x1 -> x0, waiting for transfers between devices: 43.2 us -> none  [local(): lax.psum_scatter(partial_term.astype(jnp.bfloat16), 'head', scatter_dimen...]
    dot_general x8 -> x0, matrix products: 40.7 us -> none  [the longest x4 15.8 us: attend_block(): jnp.einsum('gqk,kgd->gqd', weights, all_values, preferred_element_type=jn...]
    gather x13 -> x0, other arithmetic: 17.5 us -> none  [the longest x12 17.5 us: attend_block(): limits = jnp.concatenate([seen, jnp.zeros((1,), jnp.int32)])[key_slot]]
    dynamic_slice x28 -> x0, local copies, waits for them, and re-layouts: 14.1 us -> none  [local(): lax.map(one_block, (queries.reshape(blocks_here, BLOCK_TOKENS, query_cols...]
    sub x4 -> x0, matrix products: 12 us -> none  [attend_block(): exponent = jnp.exp(masked - row_max)]
    concatenate x24 -> x0, local copies, waits for them, and re-layouts: 9.97 us -> none  [the longest x12 8.68 us: attend_block(): jnp.concatenate([near_keys.reshape(DEPTH * BLOCK_TOKENS, kv_cols), own_ke...]
  transfers between devices with their start and end apart: 4 -> 0, of which waited for: 4 -> 0; matrix products, arithmetic and copies ran while one was open for 9% -> 0% of each run, Pallas kernels for 0% -> 0%
where the time goes in v1:
time: 70.6 us; the launch traced here: 70.3 us
  Pallas kernels  68.1 us (96%)
  local copies, waits for them, and re-layouts  2.26 us (3%)
    pallas_call x1, Pallas kernels, local(): pl.pallas_call(functools.partial(kernel, n_seq, n_head), out_shape=jax.Sh...  68.1 us
    unnamed x1, local copies, waits for them, and re-layouts  2.26 us

profile of v1, /device:TPU:0, one launch (start us, length us, event | category | flops | bytes accessed | tf_op | source)
XLA Modules:
  0.0 70.3 jit_solution(6014395797546702602)
XLA Ops:
  0.0 68.1 %shard_map.91 = bf16[512,1024]{1,0:T(8,128)(2,1)} custom-call(bf16[512,1024]{1,0:T(8,128)(2,1)} %tok_ref.1, f32[1,4096]{1,0:T(1,128)} %bitcast.1, f32[1,128]{1,0:T(1,128)} %constant.2.clone.freq_ref, bf16[4096,1024]{1,0:T(8,128)(2,1)} %wq_ref.1, bf16[4096,256]{1,0:T(8,128)(2,1)} %wk_ref.1, bf16[4096,256]{1,0:T(8,128)(2,1)} %wv_ref.1, ...), custom_call_target="tpu_custom_call" | custom-call | flops 12999999488 | bytes 25000000 | tf_op jit(solution)/shard_map/pallas_call | solution.py:389
  68.1 2.3 %copy.11 = bf16[512,1024]{1,0:T(8,128)(2,1)} copy(bf16[512,1024]{1,0:T(8,128)(2,1)} %shard_map.91) | data formatting | bytes 2097152

commit v2 on v1

--- a/solution.py
+++ b/solution.py
@@ -18,6 +18,7 @@
 SLOTS = DEPTH + 1
 KEYS = SLOTS * BLOCK_TOKENS
 LOG2E = 1.4426950408889634
+MASKED = -1e30
 
 
 def kernel(
@@ -41,12 +42,11 @@
     normed,
     qbuf,
     kvbuf,
-    kvcat,
-    bias,
+    kcat,
+    vcat,
     attn,
     psend,
     precv,
-    osum,
     acc,
     ysend,
     yrecv,
@@ -161,8 +161,10 @@
         slot = kvbuf.at[lax.rem(z + nz - j, nz) * nx + lax.rem(x + nx - i, nx)]
         return remote(slot, slot, kx_send.at[j, i - 1], kx_recv.at[j, i - 1], x_peer(nx - i), head)
 
-    def part_core(b):
-        return remote(psend.at[b], precv.at[b], p_send.at[b], p_recv.at[b], seq, partner)
+    def part_core(b, j):
+        return remote(
+            psend.at[b, j], precv.at[b, j], p_send.at[b, j], p_recv.at[b, j], seq, partner
+        )
 
     def part_y(b, j):
         return remote(
@@ -174,20 +176,49 @@
             y_peer(j),
         )
 
-    for b in range(blocks):
-        own_copy(b).start()
-    for i in range(4):
-        weight_copy(i).start()
-    pl.semaphore_wait(barrier, len(peers))
-    for b in range(blocks):
+    def send_tokens(b):
         for j in range(1, ny):
             tok_y(b, j).start()
         tok_core(b).start()
 
+    own_copy(0).start()
+    weight_copy(0).start()
+    weight_copy(1).start()
+
+    lane = lax.broadcasted_iota(jnp.int32, (BLOCK_TOKENS, BLOCK_TOKENS), 1)
+    row = lax.broadcasted_iota(jnp.int32, (BLOCK_TOKENS, BLOCK_TOKENS), 0)
+    identity = jnp.where(lane == row, 1.0, 0.0).astype(jnp.bfloat16)
+    causal = jnp.where(row <= lane, 0.0, MASKED).astype(jnp.bfloat16)
+
+    def fill(b, carry):
+        for k in range(q_cols // HEAD_SIZE):
+            qbuf[b, k, :, HEAD_SIZE:] = identity
+        return carry
+
+    lax.fori_loop(0, blocks, fill, 0)
+    for g in range(kv_heads):
+        kcat[g, DEPTH * BLOCK_TOKENS :, HEAD_SIZE:] = causal
+        vcat[g, :, HEAD_SIZE:] = jnp.ones((KEYS, HEAD_SIZE), jnp.bfloat16)
+
+    pl.semaphore_wait(barrier, len(peers))
+    send_tokens(0)
+    weight_copy(2).start()
+    for b in range(1, blocks):
+        own_copy(b).start()
+
     def project(b, carry):
         for j in range(1, ny):
             tok_y_in(b, j).wait_recv()
             tok_fwd(b, j).start()
+
+        @pl.when(b < blocks - 1)
+        def _():
+            send_tokens(b + 1)
+
+        @pl.when(b == 1)
+        def _():
+            weight_copy(3).start()
+
         own_copy(b).wait()
         tok_core_in(b).wait_recv()
 
@@ -216,7 +247,6 @@
             base += vis_ref[b, j]
         position = base + lax.broadcasted_iota(jnp.int32, (BLOCK_TOKENS, HEAD_SIZE), 0)
         angle = position.astype(jnp.float32) * freq_ref[...]
-        lane = lax.broadcasted_iota(jnp.int32, (BLOCK_TOKENS, HEAD_SIZE), 1)
         cosine = jnp.cos(angle)
         sine = jnp.sin(angle)
         sine = jnp.where(lane < HEAD_SIZE // 2, -sine, sine)
@@ -251,7 +281,9 @@
             found = jnp.dot(normed[...], wq[:, cols], preferred_element_type=jnp.float32)
             for k in range(2):
                 turned = rope(found[:, k * HEAD_SIZE : (k + 1) * HEAD_SIZE])
-                qbuf[b, 2 * t + k] = (turned * (HEAD_SIZE**-0.5 * LOG2E)).astype(jnp.bfloat16)
+                qbuf[b, 2 * t + k, :, :HEAD_SIZE] = (turned * (HEAD_SIZE**-0.5 * LOG2E)).astype(
+                    jnp.bfloat16
+                )
             return inner
 
         lax.fori_loop(0, q_cols // tile, query_tile, 0)
@@ -265,78 +297,82 @@
             kv_x_in(j, i).wait_recv()
 
     def attend(b, carry):
-        lane = lax.broadcasted_iota(jnp.int32, (BLOCK_TOKENS, BLOCK_TOKENS), 1)
-        row = lax.broadcasted_iota(jnp.int32, (BLOCK_TOKENS, BLOCK_TOKENS), 0)
         for j in range(SLOTS):
             part = slice(j * BLOCK_TOKENS, (j + 1) * BLOCK_TOKENS)
             if j < DEPTH:
                 block_id = jnp.maximum(anc_ref[b, j], 0)
                 owner, inside = lax.div(block_id, blocks), lax.rem(block_id, blocks)
                 slot = jnp.where(owner == seq, n_seq + inside, owner)
-                allowed = lane < vis_ref[b, j]
+                mask = jnp.where(row < vis_ref[b, j], 0.0, MASKED).astype(jnp.bfloat16)
             else:
                 slot = n_seq + b
-                allowed = lane <= row
-            kvcat[part] = kvbuf[slot]
-            bias[:, part] = jnp.where(allowed, 0.0, -1e30)
+            for g in range(kv_heads):
+                cols = slice(g * HEAD_SIZE, (g + 1) * HEAD_SIZE)
+                kcat[g, part, :HEAD_SIZE] = kvbuf[slot, :, cols]
+                cols = slice(kv_cols + g * HEAD_SIZE, kv_cols + (g + 1) * HEAD_SIZE)
+                vcat[g, part, :HEAD_SIZE] = kvbuf[slot, :, cols]
+                if j < DEPTH:
+                    kcat[g, part, HEAD_SIZE:] = mask
 
         for g in range(kv_heads):
             query = qbuf[b, g * group : (g + 1) * group].reshape(
-                group * BLOCK_TOKENS, HEAD_SIZE
+                group * BLOCK_TOKENS, 2 * HEAD_SIZE
             )
-            key = kvcat[:, g * HEAD_SIZE : (g + 1) * HEAD_SIZE]
-            value = kvcat[:, kv_cols + g * HEAD_SIZE : kv_cols + (g + 1) * HEAD_SIZE]
             scores = lax.dot_general(
-                query, key, (((1,), (1,)), ((), ())), preferred_element_type=jnp.float32
+                query, kcat[g], (((1,), (1,)), ((), ())), preferred_element_type=jnp.float32
             )
-            scores = (
-                scores.reshape(group, BLOCK_TOKENS, KEYS) + bias[...][None]
-            ).reshape(group * BLOCK_TOKENS, KEYS)
             top = jnp.max(scores, axis=1, keepdims=True)
-            weight = jnp.exp2(scores - top)
-            total = jnp.sum(weight, axis=1, keepdims=True)
-            mixed = jnp.dot(
-                weight.astype(jnp.bfloat16), value, preferred_element_type=jnp.float32
-            )
-            mixed = (mixed / total).astype(jnp.bfloat16)
+            weight = jnp.exp2(scores - top).astype(jnp.bfloat16)
+            mixed = jnp.dot(weight, vcat[g], preferred_element_type=jnp.float32)
+            mixed = (mixed[:, :HEAD_SIZE] / mixed[:, HEAD_SIZE:]).astype(jnp.bfloat16)
             for k in range(group):
                 at = (g * group + k) * HEAD_SIZE
                 attn[:, at : at + HEAD_SIZE] = mixed[k * BLOCK_TOKENS : (k + 1) * BLOCK_TOKENS]
 
         tile = 512
-        per = width // tile
-
-        def other_tile(t, inner):
-            k, m = lax.div(t, per), lax.rem(t, per)
-            cols = pl.ds(pl.multiple_of((2 * k + 1 - core) * width + m * tile, tile), tile)
-            into = pl.ds(pl.multiple_of(m * tile, tile), tile)
-            found = jnp.dot(attn[...], wo[:, cols], preferred_element_type=jnp.float32)
-            psend[b, k, :, into] = found.astype(jnp.bfloat16)
-            return inner
-
-        lax.fori_loop(0, ny * per, other_tile, 0)
-        part_core(b).start()
-
-        def own_tile(t, inner):
-            k, m = lax.div(t, per), lax.rem(t, per)
-            cols = pl.ds(pl.multiple_of((2 * k + core) * width + m * tile, tile), tile)
-            into = pl.ds(pl.multiple_of(m * tile, tile), tile)
-            osum[k, :, into] = jnp.dot(attn[...], wo[:, cols], preferred_element_type=jnp.float32)
-            return inner
-
-        lax.fori_loop(0, ny * per, own_tile, 0)
-        part_core(b).wait_recv()
-        for j in range(1, ny):
-            k = lax.rem(y + j, ny)
-            ysend[b, j - 1] = (osum[k] + precv[b, k].astype(jnp.float32)).astype(jnp.bfloat16)
+
+        def share(j, side, store):
+            base = (2 * lax.rem(y + j, ny) + side) * width
+
+            def one_tile(t, inner):
+                cols = pl.ds(pl.multiple_of(base + t * tile, tile), tile)
+                into = pl.ds(pl.multiple_of(t * tile, tile), tile)
+                store(into, jnp.dot(attn[...], wo[:, cols], preferred_element_type=jnp.float32))
+                return inner
+
+            lax.fori_loop(0, width // tile, one_tile, 0)
+
+        def other_share(j):
+            def store(into, found):
+                psend[b, j, :, into] = found.astype(jnp.bfloat16)
+
+            share(j, 1 - core, store)
+            part_core(b, j).start()
+
+        for j in range(1, ny):
+            other_share(j)
+        for j in range(1, ny):
+
+            def add(into, found):
+                acc[b, :, into] = found
+
+            share(j, core, add)
+            part_core(b, j).wait_recv()
+            ysend[b, j - 1] = (acc[b] + precv[b, j].astype(jnp.float32)).astype(jnp.bfloat16)
             part_y(b, j).start()
-        acc[b] = osum[y] + precv[b, y].astype(jnp.float32)
+        other_share(0)
+
+        def keep(into, found):
+            acc[b, :, into] = found
+
+        share(0, core, keep)
         return carry
 
     lax.fori_loop(0, blocks, attend, 0)
 
     def finish(b, carry):
-        result = acc[b]
+        part_core(b, 0).wait_recv()
+        result = acc[b] + precv[b, 0].astype(jnp.float32)
         for j in range(1, ny):
             part_y(b, j).wait_recv()
             result += yrecv[b, j - 1].astype(jnp.float32)
@@ -348,7 +384,8 @@
             tok_fwd(b, j).wait_send()
             part_y(b, j).wait_send()
         tok_core(b).wait_send()
-        part_core(b).wait_send()
+        for j in range(ny):
+            part_core(b, j).wait_send()
         return carry
 
     lax.fori_loop(0, blocks, finish, 0)
@@ -398,14 +435,13 @@
             pltpu.VMEM(value_weight.shape, bf16),
             pltpu.VMEM(w_out.shape, bf16),
             pltpu.VMEM((BLOCK_TOKENS, n_head * width), bf16),
-            pltpu.VMEM((blocks, q_cols // HEAD_SIZE, BLOCK_TOKENS, HEAD_SIZE), bf16),
+            pltpu.VMEM((blocks, q_cols // HEAD_SIZE, BLOCK_TOKENS, 2 * HEAD_SIZE), bf16),
             pltpu.VMEM((n_seq + blocks, BLOCK_TOKENS, 2 * kv_cols), bf16),
-            pltpu.VMEM((KEYS, 2 * kv_cols), bf16),
-            pltpu.VMEM((BLOCK_TOKENS, KEYS), f32),
+            pltpu.VMEM((kv_cols // HEAD_SIZE, KEYS, 2 * HEAD_SIZE), bf16),
+            pltpu.VMEM((kv_cols // HEAD_SIZE, KEYS, 2 * HEAD_SIZE), bf16),
             pltpu.VMEM((BLOCK_TOKENS, q_cols), bf16),
             pltpu.VMEM((blocks, ny, BLOCK_TOKENS, width), bf16),
             pltpu.VMEM((blocks, ny, BLOCK_TOKENS, width), bf16),
-            pltpu.VMEM((ny, BLOCK_TOKENS, width), f32),
             pltpu.VMEM((blocks, BLOCK_TOKENS, width), f32),
             pltpu.VMEM((blocks, ny - 1, BLOCK_TOKENS, width), bf16),
             pltpu.VMEM((blocks, ny - 1, BLOCK_TOKENS, width), bf16),
@@ -421,8 +457,8 @@
             dma((nz - 1,)),
             dma((nz, nx - 1)),
             dma((nz, nx - 1)),
-            dma((blocks,)),
-            dma((blocks,)),
+            dma((blocks, ny)),
+            dma((blocks, ny)),
             dma((blocks, ny - 1)),
             dma((blocks, ny - 1)),
         ],

time: 70.6 us -> 71.6 us (1.014)
  Pallas kernels: 68.1 us -> 69.1 us
    pallas_call x1, Pallas kernels: 68.1 us -> 69.1 us  [local(): pl.pallas_call(functools.partial(kernel, n_seq, n_head), out_shape=jax.Sh...]
where the time goes in v2:
time: 71.6 us; the launch traced here: 71.4 us
  Pallas kernels  69.1 us (97%)
  local copies, waits for them, and re-layouts  2.26 us (3%)
    pallas_call x1, Pallas kernels, local(): pl.pallas_call(functools.partial(kernel, n_seq, n_head), out_shape=jax.Sh...  69.1 us
    unnamed x1, local copies, waits for them, and re-layouts  2.26 us

profile of v2, /device:TPU:0, one launch (start us, length us, event | category | flops | bytes accessed | tf_op | source)
XLA Modules:
  0.0 71.4 jit_solution(17435348388563185192)
XLA Ops:
  0.0 69.1 %shard_map.91 = bf16[512,1024]{1,0:T(8,128)(2,1)} custom-call(bf16[512,1024]{1,0:T(8,128)(2,1)} %tok_ref.1, f32[1,4096]{1,0:T(1,128)} %bitcast.1, f32[1,128]{1,0:T(1,128)} %constant.2.clone.freq_ref, bf16[4096,1024]{1,0:T(8,128)(2,1)} %wq_ref.1, bf16[4096,256]{1,0:T(8,128)(2,1)} %wk_ref.1, bf16[4096,256]{1,0:T(8,128)(2,1)} %wv_ref.1, ...), custom_call_target="tpu_custom_call" | custom-call | flops 12999999488 | bytes 25000000 | tf_op jit(solution)/shard_map/pallas_call | solution.py:426
  69.1 2.3 %copy.11 = bf16[512,1024]{1,0:T(8,128)(2,1)} copy(bf16[512,1024]{1,0:T(8,128)(2,1)} %shard_map.91) | data formatting | bytes 2097152

commit v3 on v2

--- a/solution.py
+++ b/solution.py
@@ -39,7 +39,11 @@
     wk,
     wv,
     wo,
-    normed,
+    scaled,
+    part,
+    square,
+    cosine,
+    sine,
     qbuf,
     kvbuf,
     kcat,
@@ -51,6 +55,7 @@
     ysend,
     yrecv,
     w_sem,
+    o_sem,
     own_sem,
     ty_send,
     ty_recv,
@@ -69,8 +74,8 @@
 ):
     rows, width = tok_ref.shape
     blocks = rows // BLOCK_TOKENS
-    q_cols = wq.shape[1]
-    kv_cols = wk.shape[1]
+    q_cols = wq.shape[2]
+    kv_cols = wk.shape[2]
     kv_heads = kv_cols // HEAD_SIZE
     group = q_cols // kv_cols
     ny = n_head // 2
@@ -109,57 +114,87 @@
     for peer in peers:
         pl.semaphore_signal(barrier, inc=1, device_id=peer, device_id_type=MESH)
 
-    def weight_copy(i):
-        source = (wk_ref, wv_ref, wq_ref, wo_ref)[i]
-        return pltpu.make_async_copy(source, (wk, wv, wq, wo)[i], w_sem.at[i])
-
-    def token_rows(b):
-        return tok_ref.at[pl.ds(pl.multiple_of(b * BLOCK_TOKENS, BLOCK_TOKENS), BLOCK_TOKENS)]
-
-    def own_copy(b):
-        return pltpu.make_async_copy(token_rows(b), xbuf.at[b, head], own_sem.at[b])
+    def weight_copy(i, j):
+        source = (wk_ref, wv_ref, wq_ref)[i]
+        first = pl.multiple_of(2 * width * lax.rem(y + j, ny), 2 * width)
+        return pltpu.make_async_copy(
+            source.at[pl.ds(first, 2 * width)], (wk, wv, wq)[i].at[j], w_sem.at[i, j]
+        )
+
+    def out_copy():
+        return pltpu.make_async_copy(wo_ref, wo, o_sem)
+
+    def block_rows(b):
+        return pl.ds(pl.multiple_of(b * BLOCK_TOKENS, BLOCK_TOKENS), BLOCK_TOKENS)
+
+    def own_copy():
+        return pltpu.make_async_copy(tok_ref, xbuf.at[0, core], own_sem)
 
     def tok_y(b, j):
         return remote(
-            token_rows(b), xbuf.at[b, head], ty_send.at[b, j - 1], ty_recv.at[b, j - 1], seq, y_peer(j)
-        )
-
-    def tok_y_in(b, j):
-        slot = xbuf.at[b, y_peer(ny - j)]
-        return remote(slot, slot, ty_send.at[b, j - 1], ty_recv.at[b, j - 1], seq, y_peer(ny - j))
-
-    def tok_core(b):
-        return remote(token_rows(b), xbuf.at[b, head], tc_send.at[b], tc_recv.at[b], seq, partner)
-
-    def tok_core_in(b):
-        slot = xbuf.at[b, partner]
-        return remote(slot, slot, tc_send.at[b], tc_recv.at[b], seq, partner)
+            tok_ref.at[block_rows(b)],
+            xbuf.at[ny - j, core, block_rows(b)],
+            ty_send.at[b, j - 1],
+            ty_recv.at[b, j - 1],
+            seq,
+            y_peer(j),
+        )
+
+    def tok_core():
+        return remote(tok_ref, xbuf.at[0, core], tc_send, tc_recv, seq, partner)
+
+    def tok_core_in():
+        slot = xbuf.at[0, 1 - core]
+        return remote(slot, slot, tc_send, tc_recv, seq, partner)
 
     def tok_fwd(b, j):
-        slot = xbuf.at[b, y_peer(ny - j)]
+        slot = xbuf.at[ny - j, core, block_rows(b)]
         return remote(slot, slot, tf_send.at[b, j - 1], tf_recv.at[b, j - 1], seq, partner)
 
     def tok_fwd_in(b, j):
-        slot = xbuf.at[b, 2 * lax.rem(y + ny - j, ny) + 1 - core]
+        slot = xbuf.at[ny - j, 1 - core, block_rows(b)]
         return remote(slot, slot, tf_send.at[b, j - 1], tf_recv.at[b, j - 1], seq, partner)
 
-    def kv_z(j):
+    def kv_z(to):
         return remote(
-            kvbuf.at[n_seq], kvbuf.at[seq], kz_send.at[j - 1], kz_recv.at[j - 1], z_peer(j), head
-        )
-
-    def kv_z_in(j):
-        slot = kvbuf.at[z_peer(nz - j)]
-        return remote(slot, slot, kz_send.at[j - 1], kz_recv.at[j - 1], z_peer(nz - j), head)
-
-    def kv_x(j, i):
-        src = kvbuf.at[n_seq] if j == 0 else kvbuf.at[z_peer(nz - j)]
-        dst = kvbuf.at[seq] if j == 0 else kvbuf.at[z_peer(nz - j)]
-        return remote(src, dst, kx_send.at[j, i - 1], kx_recv.at[j, i - 1], x_peer(i), head)
-
-    def kv_x_in(j, i):
-        slot = kvbuf.at[lax.rem(z + nz - j, nz) * nx + lax.rem(x + nx - i, nx)]
-        return remote(slot, slot, kx_send.at[j, i - 1], kx_recv.at[j, i - 1], x_peer(nx - i), head)
+            kvbuf.at[n_seq], kvbuf.at[seq], kz_send.at[to], kz_recv.at[z], to * nx + x, head
+        )
+
+    def kv_z_in(source):
+        slot = kvbuf.at[source * nx + x]
+        return remote(slot, slot, kz_send.at[source], kz_recv.at[source], source * nx + x, head)
+
+    def kv_x(source, i, own):
+        slot = kvbuf.at[source * nx + x]
+        src = kvbuf.at[n_seq] if own else slot
+        return remote(
+            src, slot, kx_send.at[source, i - 1], kx_recv.at[source, i - 1], x_peer(i), head
+        )
+
+    def kv_x_in(source, i):
+        slot = kvbuf.at[source * nx + lax.rem(x + nx - i, nx)]
+        return remote(
+            slot, slot, kx_send.at[source, i - 1], kx_recv.at[source, i - 1], x_peer(nx - i), head
+        )
+
+    def along_z(distances, act):
+        for d in distances:
+
+            @pl.when(z + d < nz)
+            def _():
+                act(z + d)
+
+            @pl.when(z - d >= 0)
+            def _():
+                act(z - d)
+
+    def kv_forward(distances):
+        def pass_on(source):
+            kv_z_in(source).wait_recv()
+            for i in range(1, nx):
+                kv_x(source, i, False).start()
+
+        along_z(distances, pass_on)
 
     def part_core(b, j):
         return remote(
@@ -179,11 +214,10 @@
     def send_tokens(b):
         for j in range(1, ny):
             tok_y(b, j).start()
-        tok_core(b).start()
-
-    own_copy(0).start()
-    weight_copy(0).start()
-    weight_copy(1).start()
+
+    own_copy().start()
+    for i in range(3):
+        weight_copy(i, 0).start()
 
     lane = lax.broadcasted_iota(jnp.int32, (BLOCK_TOKENS, BLOCK_TOKENS), 1)
     row = lax.broadcasted_iota(jnp.int32, (BLOCK_TOKENS, BLOCK_TOKENS), 0)
@@ -201,84 +235,120 @@
         vcat[g, :, HEAD_SIZE:] = jnp.ones((KEYS, HEAD_SIZE), jnp.bfloat16)
 
     pl.semaphore_wait(barrier, len(peers))
+    tok_core().start()
     send_tokens(0)
-    weight_copy(2).start()
-    for b in range(1, blocks):
-        own_copy(b).start()
+    for j in range(1, ny):
+        for i in range(3):
+            weight_copy(i, j).start()
+
+    def angles(b, carry):
+        base = vis_ref[b, 0]
+        for j in range(1, DEPTH):
+            base += vis_ref[b, j]
+        angle = (base + row).astype(jnp.float32) * freq_ref[...]
+        cosine[b] = jnp.cos(angle)
+        turn = jnp.sin(angle)
+        sine[b] = jnp.where(lane < HEAD_SIZE // 2, -turn, turn)
+        return carry
+
+    lax.fori_loop(0, blocks, angles, 0)
+
+    def scale_rows(b, j):
+        total = jnp.zeros((BLOCK_TOKENS, 1), jnp.float32)
+        for c in range(2):
+            piece = xbuf[j, c, block_rows(b)].astype(jnp.float32)
+            first = (2 * lax.rem(y + j, ny) + c) * width
+            gain = gain_ref[:, pl.ds(pl.multiple_of(first, width), width)]
+            scaled[block_rows(b), c * width : (c + 1) * width] = (piece * gain).astype(jnp.bfloat16)
+            total += jnp.sum(piece * piece, axis=1, keepdims=True)
+        return jnp.broadcast_to(total, (BLOCK_TOKENS, HEAD_SIZE))
+
+    own_copy().wait()
+    tok_core_in().wait_recv()
+
+    def scale_own(b, carry):
+        square[b] = scale_rows(b, 0)
+        return carry
+
+    lax.fori_loop(0, blocks, scale_own, 0)
+    for i in range(3):
+        weight_copy(i, 0).wait()
+    part[:, q_cols : q_cols + kv_cols] = jnp.dot(
+        scaled[...], wk[0], preferred_element_type=jnp.float32
+    )
+    part[:, q_cols + kv_cols :] = jnp.dot(scaled[...], wv[0], preferred_element_type=jnp.float32)
+    tile = 2 * HEAD_SIZE
+
+    def own_tile(t, carry):
+        cols = pl.ds(pl.multiple_of(t * tile, tile), tile)
+        part[:, cols] = jnp.dot(scaled[...], wq[0, :, cols], preferred_element_type=jnp.float32)
+        return carry
+
+    lax.fori_loop(0, q_cols // tile, own_tile, 0)
 
     def project(b, carry):
         for j in range(1, ny):
-            tok_y_in(b, j).wait_recv()
+            tok_y(b, j).wait_recv()
             tok_fwd(b, j).start()
 
         @pl.when(b < blocks - 1)
         def _():
             send_tokens(b + 1)
 
-        @pl.when(b == 1)
-        def _():
-            weight_copy(3).start()
-
-        own_copy(b).wait()
-        tok_core_in(b).wait_recv()
-
-        @pl.when(b == 2)
-        def _():
-            for j in range(1, nz):
-                kv_z_in(j).wait_recv()
-                for i in range(1, nx):
-                    kv_x(j, i).start()
-
-        for j in range(1, ny):
-            tok_fwd_in(b, j).wait_recv()
-
-        square = jnp.zeros((BLOCK_TOKENS, 1), jnp.float32)
-        for k in range(n_head):
-            piece = xbuf[b, k].astype(jnp.float32)
-            square += jnp.sum(piece * piece, axis=1, keepdims=True)
-        scale = lax.rsqrt(square / (n_head * width) + NORM_EPS)
-        for k in range(n_head):
-            piece = xbuf[b, k].astype(jnp.float32)
-            cols = slice(k * width, (k + 1) * width)
-            normed[:, cols] = (piece * scale * gain_ref[:, cols]).astype(jnp.bfloat16)
-
-        base = vis_ref[b, 0]
-        for j in range(1, DEPTH):
-            base += vis_ref[b, j]
-        position = base + lax.broadcasted_iota(jnp.int32, (BLOCK_TOKENS, HEAD_SIZE), 0)
-        angle = position.astype(jnp.float32) * freq_ref[...]
-        cosine = jnp.cos(angle)
-        sine = jnp.sin(angle)
-        sine = jnp.where(lane < HEAD_SIZE // 2, -sine, sine)
-
-        def rope(vectors):
-            return vectors * cosine + pltpu.roll(vectors, HEAD_SIZE // 2, 1) * sine
-
         @pl.when(b == 0)
         def _():
-            weight_copy(0).wait()
-            weight_copy(1).wait()
-
-        keys = jnp.dot(normed[...], wk[...], preferred_element_type=jnp.float32)
+            out_copy().start()
+            for j in range(1, ny):
+                for i in range(3):
+                    weight_copy(i, j).wait()
+
+        rows_b = block_rows(b)
+
+        def add_far(first, weight, cols, j):
+            into = (rows_b, pl.ds(first, cols))
+            part[into] += jnp.dot(scaled[rows_b], weight, preferred_element_type=jnp.float32)
+
+        for j in range(1, ny):
+            tok_fwd_in(b, j).wait_recv()
+            square[b] += scale_rows(b, j)
+            add_far(q_cols, wk[j], kv_cols, j)
+            add_far(q_cols + kv_cols, wv[j], kv_cols, j)
+            if j < ny - 1:
+
+                def far_tile(t, inner):
+                    first = pl.multiple_of(t * tile, tile)
+                    add_far(first, wq[j, :, pl.ds(first, tile)], tile, j)
+                    return inner
+
+                lax.fori_loop(0, q_cols // tile, far_tile, 0)
+        scale = lax.rsqrt(square[b] / (n_head * width) + NORM_EPS)
+
+        def rope(vectors):
+            vectors = vectors * scale
+            return vectors * cosine[b] + pltpu.roll(vectors, HEAD_SIZE // 2, 1) * sine[b]
+
         for g in range(kv_heads):
             cols = slice(g * HEAD_SIZE, (g + 1) * HEAD_SIZE)
-            kvbuf[n_seq + b, :, cols] = rope(keys[:, cols]).astype(jnp.bfloat16)
-        values = jnp.dot(normed[...], wv[...], preferred_element_type=jnp.float32)
-        kvbuf[n_seq + b, :, kv_cols:] = values.astype(jnp.bfloat16)
+            at = q_cols + g * HEAD_SIZE
+            kvbuf[n_seq + b, :, cols] = rope(part[rows_b, at : at + HEAD_SIZE]).astype(jnp.bfloat16)
+            at += kv_cols
+            cols = slice(kv_cols + g * HEAD_SIZE, kv_cols + (g + 1) * HEAD_SIZE)
+            kvbuf[n_seq + b, :, cols] = (part[rows_b, at : at + HEAD_SIZE] * scale).astype(
+                jnp.bfloat16
+            )
 
         @pl.when(b == 0)
         def _():
-            for j in range(1, nz):
-                kv_z(j).start()
             for i in range(1, nx):
-                kv_x(0, i).start()
-            weight_copy(2).wait()
-
-        tile = 2 * HEAD_SIZE
+                kv_x(z, i, True).start()
+            along_z(range(1, nz), lambda to: kv_z(to).start())
 
         def query_tile(t, inner):
-            cols = pl.ds(pl.multiple_of(t * tile, tile), tile)
-            found = jnp.dot(normed[...], wq[:, cols], preferred_element_type=jnp.float32)
+            first = pl.multiple_of(t * tile, tile)
+            cols = pl.ds(first, tile)
+            found = part[rows_b, cols] + jnp.dot(
+                scaled[rows_b], wq[ny - 1, :, cols], preferred_element_type=jnp.float32
+            )
             for k in range(2):
                 turned = rope(found[:, k * HEAD_SIZE : (k + 1) * HEAD_SIZE])
                 qbuf[b, 2 * t + k, :, :HEAD_SIZE] = (turned * (HEAD_SIZE**-0.5 * LOG2E)).astype(
@@ -287,18 +357,27 @@
             return inner
 
         lax.fori_loop(0, q_cols // tile, query_tile, 0)
+
+        @pl.when(b == 1)
+        def _():
+            kv_forward(range(1, 2))
+
+        @pl.when(b == 2)
+        def _():
+            kv_forward(range(2, nz))
+
         return carry
 
     lax.fori_loop(0, blocks, project, 0)
 
-    weight_copy(3).wait()
-    for j in range(nz):
+    out_copy().wait()
+    for source in range(nz):
         for i in range(1, nx):
-            kv_x_in(j, i).wait_recv()
+            kv_x_in(source, i).wait_recv()
 
     def attend(b, carry):
         for j in range(SLOTS):
-            part = slice(j * BLOCK_TOKENS, (j + 1) * BLOCK_TOKENS)
+            span = slice(j * BLOCK_TOKENS, (j + 1) * BLOCK_TOKENS)
             if j < DEPTH:
                 block_id = jnp.maximum(anc_ref[b, j], 0)
                 owner, inside = lax.div(block_id, blocks), lax.rem(block_id, blocks)
@@ -308,11 +387,11 @@
                 slot = n_seq + b
             for g in range(kv_heads):
                 cols = slice(g * HEAD_SIZE, (g + 1) * HEAD_SIZE)
-                kcat[g, part, :HEAD_SIZE] = kvbuf[slot, :, cols]
+                kcat[g, span, :HEAD_SIZE] = kvbuf[slot, :, cols]
                 cols = slice(kv_cols + g * HEAD_SIZE, kv_cols + (g + 1) * HEAD_SIZE)
-                vcat[g, part, :HEAD_SIZE] = kvbuf[slot, :, cols]
+                vcat[g, span, :HEAD_SIZE] = kvbuf[slot, :, cols]
                 if j < DEPTH:
-                    kcat[g, part, HEAD_SIZE:] = mask
+                    kcat[g, span, HEAD_SIZE:] = mask
 
         for g in range(kv_heads):
             query = qbuf[b, g * group : (g + 1) * group].reshape(
@@ -383,17 +462,16 @@
             tok_y(b, j).wait_send()
             tok_fwd(b, j).wait_send()
             part_y(b, j).wait_send()
-        tok_core(b).wait_send()
         for j in range(ny):
             part_core(b, j).wait_send()
         return carry
 
     lax.fori_loop(0, blocks, finish, 0)
-    for j in range(1, nz):
-        kv_z(j).wait_send()
-    for j in range(nz):
+    tok_core().wait_send()
+    along_z(range(1, nz), lambda to: kv_z(to).wait_send())
+    for source in range(nz):
         for i in range(1, nx):
-            kv_x(j, i).wait_send()
+            kv_x(source, i, True).wait_send()
 
 
 def local(
@@ -429,12 +507,16 @@
         in_specs=[hbm, vmem, vmem, hbm, hbm, hbm, hbm, smem, smem],
         out_specs=vmem,
         scratch_shapes=[
-            pltpu.VMEM((blocks, n_head, BLOCK_TOKENS, width), bf16),
-            pltpu.VMEM(w_query.shape, bf16),
-            pltpu.VMEM(key_weight.shape, bf16),
-            pltpu.VMEM(value_weight.shape, bf16),
+            pltpu.VMEM((ny, 2, rows, width), bf16),
+            pltpu.VMEM((ny, 2 * width, q_cols), bf16),
+            pltpu.VMEM((ny, 2 * width, kv_cols), bf16),
+            pltpu.VMEM((ny, 2 * width, kv_cols), bf16),
             pltpu.VMEM(w_out.shape, bf16),
-            pltpu.VMEM((BLOCK_TOKENS, n_head * width), bf16),
+            pltpu.VMEM((rows, 2 * width), bf16),
+            pltpu.VMEM((rows, q_cols + 2 * kv_cols), f32),
+            pltpu.VMEM((blocks, BLOCK_TOKENS, HEAD_SIZE), f32),
+            pltpu.VMEM((blocks, BLOCK_TOKENS, HEAD_SIZE), f32),
+            pltpu.VMEM((blocks, BLOCK_TOKENS, HEAD_SIZE), f32),
             pltpu.VMEM((blocks, q_cols // HEAD_SIZE, BLOCK_TOKENS, 2 * HEAD_SIZE), bf16),
             pltpu.VMEM((n_seq + blocks, BLOCK_TOKENS, 2 * kv_cols), bf16),
             pltpu.VMEM((kv_cols // HEAD_SIZE, KEYS, 2 * HEAD_SIZE), bf16),
@@ -445,16 +527,17 @@
             pltpu.VMEM((blocks, BLOCK_TOKENS, width), f32),
             pltpu.VMEM((blocks, ny - 1, BLOCK_TOKENS, width), bf16),
             pltpu.VMEM((blocks, ny - 1, BLOCK_TOKENS, width), bf16),
-            dma((4,)),
-            dma((blocks,)),
+            dma((3, ny)),
+            dma,
+            dma,
             dma((blocks, ny - 1)),
             dma((blocks, ny - 1)),
-            dma((blocks,)),
-            dma((blocks,)),
+            dma,
+            dma,
             dma((blocks, ny - 1)),
             dma((blocks, ny - 1)),
-            dma((nz - 1,)),
-            dma((nz - 1,)),
+            dma((nz,)),
+            dma((nz,)),
             dma((nz, nx - 1)),
             dma((nz, nx - 1)),
             dma((blocks, ny)),

time: 71.6 us -> 74.8 us (1.045)
  Pallas kernels: 69.1 us -> 72.3 us
    pallas_call x1, Pallas kernels: 69.1 us -> 72.3 us  [local(): pl.pallas_call(functools.partial(kernel, n_seq, n_head), out_shape=jax.Sh...]
where the time goes in v3:
time: 74.8 us; the launch traced here: 74.5 us
  Pallas kernels  72.3 us (97%)
  local copies, waits for them, and re-layouts  2.26 us (3%)
    pallas_call x1, Pallas kernels, local(): pl.pallas_call(functools.partial(kernel, n_seq, n_head), out_shape=jax.Sh...  72.3 us
    unnamed x1, local copies, waits for them, and re-layouts  2.26 us

profile of v3, /device:TPU:0, one launch (start us, length us, event | category | flops | bytes accessed | tf_op | source)
XLA Modules:
  0.0 74.5 jit_solution(14342597318932250831)
XLA Ops:
  0.0 72.3 %shard_map.91 = bf16[512,1024]{1,0:T(8,128)(2,1)} custom-call(bf16[512,1024]{1,0:T(8,128)(2,1)} %tok_ref.1, f32[1,4096]{1,0:T(1,128)} %bitcast.1, f32[1,128]{1,0:T(1,128)} %constant.2.clone.freq_ref, bf16[4096,1024]{1,0:T(8,128)(2,1)} %wq_ref.1, bf16[4096,256]{1,0:T(8,128)(2,1)} %wk_ref.1, bf16[4096,256]{1,0:T(8,128)(2,1)} %wv_ref.1, ...), custom_call_target="tpu_custom_call" | custom-call | flops 12999999488 | bytes 25000000 | tf_op jit(solution)/shard_map/pallas_call | solution.py:504
  72.3 2.3 %copy.11 = bf16[512,1024]{1,0:T(8,128)(2,1)} copy(bf16[512,1024]{1,0:T(8,128)(2,1)} %shard_map.91) | data formatting | bytes 2097152

commit v4 on v3

--- a/solution.py
+++ b/solution.py
@@ -40,6 +40,7 @@
     wv,
     wo,
     scaled,
+    far,
     part,
     square,
     cosine,
@@ -235,8 +236,9 @@
         vcat[g, :, HEAD_SIZE:] = jnp.ones((KEYS, HEAD_SIZE), jnp.bfloat16)
 
     pl.semaphore_wait(barrier, len(peers))
+    send_tokens(0)
     tok_core().start()
-    send_tokens(0)
+    send_tokens(1)
     for j in range(1, ny):
         for i in range(3):
             weight_copy(i, j).start()
@@ -253,13 +255,14 @@
 
     lax.fori_loop(0, blocks, angles, 0)
 
-    def scale_rows(b, j):
+    def scale_rows(b, j, into, into_rows):
         total = jnp.zeros((BLOCK_TOKENS, 1), jnp.float32)
         for c in range(2):
             piece = xbuf[j, c, block_rows(b)].astype(jnp.float32)
             first = (2 * lax.rem(y + j, ny) + c) * width
             gain = gain_ref[:, pl.ds(pl.multiple_of(first, width), width)]
-            scaled[block_rows(b), c * width : (c + 1) * width] = (piece * gain).astype(jnp.bfloat16)
+            at = (max(j - 1, 0) * 2 + c) * width
+            into[into_rows, at : at + width] = (piece * gain).astype(jnp.bfloat16)
             total += jnp.sum(piece * piece, axis=1, keepdims=True)
         return jnp.broadcast_to(total, (BLOCK_TOKENS, HEAD_SIZE))
 
@@ -267,11 +270,11 @@
     tok_core_in().wait_recv()
 
     def scale_own(b, carry):
-        square[b] = scale_rows(b, 0)
+        square[b] = scale_rows(b, 0, scaled, block_rows(b))
         return carry
 
     lax.fori_loop(0, blocks, scale_own, 0)
-    for i in range(3):
+    for i in range(2):
         weight_copy(i, 0).wait()
     part[:, q_cols : q_cols + kv_cols] = jnp.dot(
         scaled[...], wk[0], preferred_element_type=jnp.float32
@@ -284,43 +287,33 @@
         part[:, cols] = jnp.dot(scaled[...], wq[0, :, cols], preferred_element_type=jnp.float32)
         return carry
 
-    lax.fori_loop(0, q_cols // tile, own_tile, 0)
-
-    def project(b, carry):
+    def arrive(b):
         for j in range(1, ny):
             tok_y(b, j).wait_recv()
             tok_fwd(b, j).start()
 
-        @pl.when(b < blocks - 1)
+        @pl.when(b < blocks - 2)
         def _():
-            send_tokens(b + 1)
+            send_tokens(b + 2)
 
         @pl.when(b == 0)
         def _():
             out_copy().start()
             for j in range(1, ny):
-                for i in range(3):
+                for i in range(2):
                     weight_copy(i, j).wait()
 
         rows_b = block_rows(b)
 
         def add_far(first, weight, cols, j):
             into = (rows_b, pl.ds(first, cols))
-            part[into] += jnp.dot(scaled[rows_b], weight, preferred_element_type=jnp.float32)
+            part[into] += jnp.dot(far[:, (j - 1) * 2 * width : j * 2 * width], weight, preferred_element_type=jnp.float32)
 
         for j in range(1, ny):
             tok_fwd_in(b, j).wait_recv()
-            square[b] += scale_rows(b, j)
+            square[b] += scale_rows(b, j, far, slice(None))
             add_far(q_cols, wk[j], kv_cols, j)
             add_far(q_cols + kv_cols, wv[j], kv_cols, j)
-            if j < ny - 1:
-
-                def far_tile(t, inner):
-                    first = pl.multiple_of(t * tile, tile)
-                    add_far(first, wq[j, :, pl.ds(first, tile)], tile, j)
-                    return inner
-
-                lax.fori_loop(0, q_cols // tile, far_tile, 0)
         scale = lax.rsqrt(square[b] / (n_head * width) + NORM_EPS)
 
         def rope(vectors):
@@ -342,13 +335,20 @@
             for i in range(1, nx):
                 kv_x(z, i, True).start()
             along_z(range(1, nz), lambda to: kv_z(to).start())
+            for j in range(ny):
+                weight_copy(2, j).wait()
+            lax.fori_loop(0, q_cols // tile, own_tile, 0)
 
         def query_tile(t, inner):
             first = pl.multiple_of(t * tile, tile)
             cols = pl.ds(first, tile)
-            found = part[rows_b, cols] + jnp.dot(
-                scaled[rows_b], wq[ny - 1, :, cols], preferred_element_type=jnp.float32
-            )
+            found = part[rows_b, cols]
+            for j in range(1, ny):
+                found += jnp.dot(
+                    far[:, (j - 1) * 2 * width : j * 2 * width],
+                    wq[j, :, cols],
+                    preferred_element_type=jnp.float32,
+                )
             for k in range(2):
                 turned = rope(found[:, k * HEAD_SIZE : (k + 1) * HEAD_SIZE])
                 qbuf[b, 2 * t + k, :, :HEAD_SIZE] = (turned * (HEAD_SIZE**-0.5 * LOG2E)).astype(
@@ -358,24 +358,13 @@
 
         lax.fori_loop(0, q_cols // tile, query_tile, 0)
 
-        @pl.when(b == 1)
-        def _():
-            kv_forward(range(1, 2))
-
-        @pl.when(b == 2)
-        def _():
-            kv_forward(range(2, nz))
-
-        return carry
-
-    lax.fori_loop(0, blocks, project, 0)
-
-    out_copy().wait()
-    for source in range(nz):
-        for i in range(1, nx):
-            kv_x_in(source, i).wait_recv()
-
-    def attend(b, carry):
+        for stage, distances in enumerate(((1,), (2,), range(3, nz))):
+
+            @pl.when(b == stage)
+            def _():
+                kv_forward([d for d in distances if d < nz])
+
+    def attend(b):
         for j in range(SLOTS):
             span = slice(j * BLOCK_TOKENS, (j + 1) * BLOCK_TOKENS)
             if j < DEPTH:
@@ -445,9 +434,28 @@
             acc[b, :, into] = found
 
         share(0, core, keep)
+
+    lag = 2
+
+    def step(s, carry):
+        @pl.when(s < blocks)
+        def _():
+            arrive(s)
+
+        @pl.when(s == lag)
+        def _():
+            out_copy().wait()
+            for source in range(nz):
+                for i in range(1, nx):
+                    kv_x_in(source, i).wait_recv()
+
+        @pl.when(s >= lag)
+        def _():
+            attend(s - lag)
+
         return carry
 
-    lax.fori_loop(0, blocks, attend, 0)
+    lax.fori_loop(0, blocks + lag, step, 0)
 
     def finish(b, carry):
         part_core(b, 0).wait_recv()
@@ -513,6 +521,7 @@
             pltpu.VMEM((ny, 2 * width, kv_cols), bf16),
             pltpu.VMEM(w_out.shape, bf16),
             pltpu.VMEM((rows, 2 * width), bf16),
+            pltpu.VMEM((BLOCK_TOKENS, (ny - 1) * 2 * width), bf16),
             pltpu.VMEM((rows, q_cols + 2 * kv_cols), f32),
             pltpu.VMEM((blocks, BLOCK_TOKENS, HEAD_SIZE), f32),
             pltpu.VMEM((blocks, BLOCK_TOKENS, HEAD_SIZE), f32),

time: 74.8 us -> 73.1 us (0.977)
  Pallas kernels: 72.3 us -> 70.5 us
    pallas_call x1, Pallas kernels: 72.3 us -> 70.5 us  [local(): pl.pallas_call(functools.partial(kernel, n_seq, n_head), out_shape=jax.Sh...]
where the time goes in v4:
time: 73.1 us; the launch traced here: 72.8 us
  Pallas kernels  70.5 us (96%)
  local copies, waits for them, and re-layouts  2.26 us (3%)
    pallas_call x1, Pallas kernels, local(): pl.pallas_call(functools.partial(kernel, n_seq, n_head), out_shape=jax.Sh...  70.5 us
    unnamed x1, local copies, waits for them, and re-layouts  2.26 us

profile of v4, /device:TPU:0, one launch (start us, length us, event | category | flops | bytes accessed | tf_op | source)
XLA Modules:
  0.0 72.8 jit_solution(12902802338910727)
XLA Ops:
  0.0 70.5 %shard_map.91 = bf16[512,1024]{1,0:T(8,128)(2,1)} custom-call(bf16[512,1024]{1,0:T(8,128)(2,1)} %tok_ref.1, f32[1,4096]{1,0:T(1,128)} %bitcast.1, f32[1,128]{1,0:T(1,128)} %constant.2.clone.freq_ref, bf16[4096,1024]{1,0:T(8,128)(2,1)} %wq_ref.1, bf16[4096,256]{1,0:T(8,128)(2,1)} %wk_ref.1, bf16[4096,256]{1,0:T(8,128)(2,1)} %wv_ref.1, ...), custom_call_target="tpu_custom_call" | custom-call | flops 12999999488 | bytes 25000000 | tf_op jit(solution)/shard_map/pallas_call | solution.py:512
  70.6 2.3 %copy.11 = bf16[512,1024]{1,0:T(8,128)(2,1)} copy(bf16[512,1024]{1,0:T(8,128)(2,1)} %shard_map.91) | data formatting | bytes 2097152

commit v5 on v4

--- a/solution.py
+++ b/solution.py
@@ -52,6 +52,7 @@
     attn,
     psend,
     precv,
+    far_sum,
     acc,
     ysend,
     yrecv,
@@ -223,7 +224,7 @@
     lane = lax.broadcasted_iota(jnp.int32, (BLOCK_TOKENS, BLOCK_TOKENS), 1)
     row = lax.broadcasted_iota(jnp.int32, (BLOCK_TOKENS, BLOCK_TOKENS), 0)
     identity = jnp.where(lane == row, 1.0, 0.0).astype(jnp.bfloat16)
-    causal = jnp.where(row <= lane, 0.0, MASKED).astype(jnp.bfloat16)
+    causal = jnp.where(lane <= row, 0.0, MASKED).astype(jnp.bfloat16)
 
     def fill(b, carry):
         for k in range(q_cols // HEAD_SIZE):
@@ -232,7 +233,7 @@
 
     lax.fori_loop(0, blocks, fill, 0)
     for g in range(kv_heads):
-        kcat[g, DEPTH * BLOCK_TOKENS :, HEAD_SIZE:] = causal
+        kcat[g, HEAD_SIZE:, DEPTH * BLOCK_TOKENS :] = causal
         vcat[g, :, HEAD_SIZE:] = jnp.ones((KEYS, HEAD_SIZE), jnp.bfloat16)
 
     pl.semaphore_wait(barrier, len(peers))
@@ -323,7 +324,8 @@
         for g in range(kv_heads):
             cols = slice(g * HEAD_SIZE, (g + 1) * HEAD_SIZE)
             at = q_cols + g * HEAD_SIZE
-            kvbuf[n_seq + b, :, cols] = rope(part[rows_b, at : at + HEAD_SIZE]).astype(jnp.bfloat16)
+            turned = rope(part[rows_b, at : at + HEAD_SIZE])
+            kvbuf[n_seq + b, :, cols] = turned.T.astype(jnp.bfloat16)
             at += kv_cols
             cols = slice(kv_cols + g * HEAD_SIZE, kv_cols + (g + 1) * HEAD_SIZE)
             kvbuf[n_seq + b, :, cols] = (part[rows_b, at : at + HEAD_SIZE] * scale).astype(
@@ -371,24 +373,22 @@
                 block_id = jnp.maximum(anc_ref[b, j], 0)
                 owner, inside = lax.div(block_id, blocks), lax.rem(block_id, blocks)
                 slot = jnp.where(owner == seq, n_seq + inside, owner)
-                mask = jnp.where(row < vis_ref[b, j], 0.0, MASKED).astype(jnp.bfloat16)
+                mask = jnp.where(lane < vis_ref[b, j], 0.0, MASKED).astype(jnp.bfloat16)
             else:
                 slot = n_seq + b
             for g in range(kv_heads):
                 cols = slice(g * HEAD_SIZE, (g + 1) * HEAD_SIZE)
-                kcat[g, span, :HEAD_SIZE] = kvbuf[slot, :, cols]
+                kcat[g, :HEAD_SIZE, span] = kvbuf[slot, :, cols]
                 cols = slice(kv_cols + g * HEAD_SIZE, kv_cols + (g + 1) * HEAD_SIZE)
                 vcat[g, span, :HEAD_SIZE] = kvbuf[slot, :, cols]
                 if j < DEPTH:
-                    kcat[g, span, HEAD_SIZE:] = mask
+                    kcat[g, HEAD_SIZE:, span] = mask
 
         for g in range(kv_heads):
             query = qbuf[b, g * group : (g + 1) * group].reshape(
                 group * BLOCK_TOKENS, 2 * HEAD_SIZE
             )
-            scores = lax.dot_general(
-                query, kcat[g], (((1,), (1,)), ((), ())), preferred_element_type=jnp.float32
-            )
+            scores = jnp.dot(query, kcat[g], preferred_element_type=jnp.float32)
             top = jnp.max(scores, axis=1, keepdims=True)
             weight = jnp.exp2(scores - top).astype(jnp.bfloat16)
             mixed = jnp.dot(weight, vcat[g], preferred_element_type=jnp.float32)
@@ -419,21 +419,24 @@
 
         for j in range(1, ny):
             other_share(j)
-        for j in range(1, ny):
-
-            def add(into, found):
-                acc[b, :, into] = found
-
-            share(j, core, add)
-            part_core(b, j).wait_recv()
-            ysend[b, j - 1] = (acc[b] + precv[b, j].astype(jnp.float32)).astype(jnp.bfloat16)
-            part_y(b, j).start()
         other_share(0)
+        for j in range(1, ny):
+
+            def put(into, found):
+                far_sum[j - 1, :, into] = found
+
+            share(j, core, put)
 
         def keep(into, found):
             acc[b, :, into] = found
 
         share(0, core, keep)
+        for j in range(1, ny):
+            part_core(b, j).wait_recv()
+            ysend[b, j - 1] = (far_sum[j - 1] + precv[b, j].astype(jnp.float32)).astype(
+                jnp.bfloat16
+            )
+            part_y(b, j).start()
 
     lag = 2
 
@@ -528,11 +531,12 @@
             pltpu.VMEM((blocks, BLOCK_TOKENS, HEAD_SIZE), f32),
             pltpu.VMEM((blocks, q_cols // HEAD_SIZE, BLOCK_TOKENS, 2 * HEAD_SIZE), bf16),
             pltpu.VMEM((n_seq + blocks, BLOCK_TOKENS, 2 * kv_cols), bf16),
-            pltpu.VMEM((kv_cols // HEAD_SIZE, KEYS, 2 * HEAD_SIZE), bf16),
+            pltpu.VMEM((kv_cols // HEAD_SIZE, 2 * HEAD_SIZE, KEYS), bf16),
             pltpu.VMEM((kv_cols // HEAD_SIZE, KEYS, 2 * HEAD_SIZE), bf16),
             pltpu.VMEM((BLOCK_TOKENS, q_cols), bf16),
             pltpu.VMEM((blocks, ny, BLOCK_TOKENS, width), bf16),
             pltpu.VMEM((blocks, ny, BLOCK_TOKENS, width), bf16),
+            pltpu.VMEM((ny - 1, BLOCK_TOKENS, width), f32),
             pltpu.VMEM((blocks, BLOCK_TOKENS, width), f32),
             pltpu.VMEM((blocks, ny - 1, BLOCK_TOKENS, width), bf16),
             pltpu.VMEM((blocks, ny - 1, BLOCK_TOKENS, width), bf16),

time: 73.1 us -> 72.9 us (level)
  no operation moved by 1% of the time
where the time goes in v5:
time: 72.9 us; the launch traced here: 72.7 us
  Pallas kernels  70.4 us (97%)
  local copies, waits for them, and re-layouts  2.26 us (3%)
    pallas_call x1, Pallas kernels, local(): pl.pallas_call(functools.partial(kernel, n_seq, n_head), out_shape=jax.Sh...  70.4 us
    unnamed x1, local copies, waits for them, and re-layouts  2.26 us

profile of v5, /device:TPU:0, one launch (start us, length us, event | category | flops | bytes accessed | tf_op | source)
XLA Modules:
  0.0 72.7 jit_solution(8053933294034321026)
XLA Ops:
  0.0 70.4 %shard_map.91 = bf16[512,1024]{1,0:T(8,128)(2,1)} custom-call(bf16[512,1024]{1,0:T(8,128)(2,1)} %tok_ref.1, f32[1,4096]{1,0:T(1,128)} %bitcast.1, f32[1,128]{1,0:T(1,128)} %constant.2.clone.freq_ref, bf16[4096,1024]{1,0:T(8,128)(2,1)} %wq_ref.1, bf16[4096,256]{1,0:T(8,128)(2,1)} %wk_ref.1, bf16[4096,256]{1,0:T(8,128)(2,1)} %wv_ref.1, ...), custom_call_target="tpu_custom_call" | custom-call | flops 12999999488 | bytes 25000000 | tf_op jit(solution)/shard_map/pallas_call | solution.py:515
  70.4 2.3 %copy.11 = bf16[512,1024]{1,0:T(8,128)(2,1)} copy(bf16[512,1024]{1,0:T(8,128)(2,1)} %shard_map.91) | data formatting | bytes 2097152

commit v6 on v5

--- a/solution.py
+++ b/solution.py
@@ -157,14 +157,21 @@
         slot = xbuf.at[ny - j, 1 - core, block_rows(b)]
         return remote(slot, slot, tf_send.at[b, j - 1], tf_recv.at[b, j - 1], seq, partner)
 
-    def kv_z(to):
+    def kv_own(way):
         return remote(
-            kvbuf.at[n_seq], kvbuf.at[seq], kz_send.at[to], kz_recv.at[z], to * nx + x, head
-        )
-
-    def kv_z_in(source):
+            kvbuf.at[n_seq],
+            kvbuf.at[seq],
+            kz_send.at[nz + (way + 1) // 2],
+            kz_recv.at[z],
+            (z + way) * nx + x,
+            head,
+        )
+
+    def kv_hop(source, way):
         slot = kvbuf.at[source * nx + x]
-        return remote(slot, slot, kz_send.at[source], kz_recv.at[source], source * nx + x, head)
+        return remote(
+            slot, slot, kz_send.at[source], kz_recv.at[source], (z + way) * nx + x, head
+        )
 
     def kv_x(source, i, own):
         slot = kvbuf.at[source * nx + x]
@@ -179,24 +186,33 @@
             slot, slot, kx_send.at[source, i - 1], kx_recv.at[source, i - 1], x_peer(nx - i), head
         )
 
-    def along_z(distances, act):
+    def own_z(act):
+        for way in (1, -1):
+
+            @pl.when((z + way >= 0) & (z + way < nz))
+            def _():
+                act(kv_own(way))
+
+    def along_z(distances, arrived, onward):
         for d in distances:
-
-            @pl.when(z + d < nz)
-            def _():
-                act(z + d)
-
-            @pl.when(z - d >= 0)
-            def _():
-                act(z - d)
+            for way in (1, -1):
+                source = z - way * d
+
+                @pl.when((source >= 0) & (source < nz))
+                def _():
+                    arrived(source, way)
+
+                    @pl.when((z + way >= 0) & (z + way < nz))
+                    def _():
+                        onward(kv_hop(source, way))
 
     def kv_forward(distances):
-        def pass_on(source):
-            kv_z_in(source).wait_recv()
+        def arrived(source, way):
+            kv_hop(source, -way).wait_recv()
             for i in range(1, nx):
                 kv_x(source, i, False).start()
 
-        along_z(distances, pass_on)
+        along_z(distances, arrived, lambda copy: copy.start())
 
     def part_core(b, j):
         return remote(
@@ -336,7 +352,7 @@
         def _():
             for i in range(1, nx):
                 kv_x(z, i, True).start()
-            along_z(range(1, nz), lambda to: kv_z(to).start())
+            own_z(lambda copy: copy.start())
             for j in range(ny):
                 weight_copy(2, j).wait()
             lax.fori_loop(0, q_cols // tile, own_tile, 0)
@@ -479,7 +495,8 @@
 
     lax.fori_loop(0, blocks, finish, 0)
     tok_core().wait_send()
-    along_z(range(1, nz), lambda to: kv_z(to).wait_send())
+    own_z(lambda copy: copy.wait_send())
+    along_z(range(1, nz), lambda source, way: None, lambda copy: copy.wait_send())
     for source in range(nz):
         for i in range(1, nx):
             kv_x(source, i, True).wait_send()
@@ -549,7 +566,7 @@
             dma,
             dma((blocks, ny - 1)),
             dma((blocks, ny - 1)),
-            dma((nz,)),
+            dma((nz + 2,)),
             dma((nz,)),
             dma((nz, nx - 1)),
             dma((nz, nx - 1)),

time: 72.9 us -> 70.8 us (0.971)
  Pallas kernels: 70.4 us -> 68.3 us
    pallas_call x1, Pallas kernels: 70.4 us -> 68.3 us  [local(): pl.pallas_call(functools.partial(kernel, n_seq, n_head), out_shape=jax.Sh...]
where the time goes in v6:
time: 70.8 us; the launch traced here: 70.5 us
  Pallas kernels  68.3 us (96%)
  local copies, waits for them, and re-layouts  2.26 us (3%)
    pallas_call x1, Pallas kernels, local(): pl.pallas_call(functools.partial(kernel, n_seq, n_head), out_shape=jax.Sh...  68.3 us
    unnamed x1, local copies, waits for them, and re-layouts  2.26 us

profile of v6, /device:TPU:0, one launch (start us, length us, event | category | flops | bytes accessed | tf_op | source)
XLA Modules:
  0.0 70.5 jit_solution(14366006023321456980)
XLA Ops:
  0.0 68.3 %shard_map.91 = bf16[512,1024]{1,0:T(8,128)(2,1)} custom-call(bf16[512,1024]{1,0:T(8,128)(2,1)} %tok_ref.1, f32[1,4096]{1,0:T(1,128)} %bitcast.1, f32[1,128]{1,0:T(1,128)} %constant.2.clone.freq_ref, bf16[4096,1024]{1,0:T(8,128)(2,1)} %wq_ref.1, bf16[4096,256]{1,0:T(8,128)(2,1)} %wk_ref.1, bf16[4096,256]{1,0:T(8,128)(2,1)} %wv_ref.1, ...), custom_call_target="tpu_custom_call" | custom-call | flops 12999999488 | bytes 25000000 | tf_op jit(solution)/shard_map/pallas_call | solution.py:532
  68.3 2.3 %copy.11 = bf16[512,1024]{1,0:T(8,128)(2,1)} copy(bf16[512,1024]{1,0:T(8,128)(2,1)} %shard_map.91) | data formatting | bytes 2097152

commit v7 on v6

--- a/solution.py
+++ b/solution.py
@@ -255,7 +255,8 @@
     pl.semaphore_wait(barrier, len(peers))
     send_tokens(0)
     tok_core().start()
-    send_tokens(1)
+    for b in range(1, blocks):
+        send_tokens(b)
     for j in range(1, ny):
         for i in range(3):
             weight_copy(i, j).start()
@@ -308,10 +309,6 @@
         for j in range(1, ny):
             tok_y(b, j).wait_recv()
             tok_fwd(b, j).start()
-
-        @pl.when(b < blocks - 2)
-        def _():
-            send_tokens(b + 2)
 
         @pl.when(b == 0)
         def _():
@@ -454,7 +451,7 @@
             )
             part_y(b, j).start()
 
-    lag = 2
+    lag = 3
 
     def step(s, carry):
         @pl.when(s < blocks)

time: 70.8 us -> 67.9 us (0.959)
  Pallas kernels: 68.3 us -> 65.4 us
    pallas_call x1, Pallas kernels: 68.3 us -> 65.4 us  [local(): pl.pallas_call(functools.partial(kernel, n_seq, n_head), out_shape=jax.Sh...]
where the time goes in v7:
time: 67.9 us; the launch traced here: 67.7 us
  Pallas kernels  65.4 us (96%)
  local copies, waits for them, and re-layouts  2.26 us (3%)
    pallas_call x1, Pallas kernels, local(): pl.pallas_call(functools.partial(kernel, n_seq, n_head), out_shape=jax.Sh...  65.4 us
    unnamed x1, local copies, waits for them, and re-layouts  2.26 us

profile of v7, /device:TPU:0, one launch (start us, length us, event | category | flops | bytes accessed | tf_op | source)
XLA Modules:
  0.0 67.7 jit_solution(3840281242562104794)
XLA Ops:
  0.0 65.4 %shard_map.91 = bf16[512,1024]{1,0:T(8,128)(2,1)} custom-call(bf16[512,1024]{1,0:T(8,128)(2,1)} %tok_ref.1, f32[1,4096]{1,0:T(1,128)} %bitcast.1, f32[1,128]{1,0:T(1,128)} %constant.2.clone.freq_ref, bf16[4096,1024]{1,0:T(8,128)(2,1)} %wq_ref.1, bf16[4096,256]{1,0:T(8,128)(2,1)} %wk_ref.1, bf16[4096,256]{1,0:T(8,128)(2,1)} %wv_ref.1, ...), custom_call_target="tpu_custom_call" | custom-call | flops 12999999488 | bytes 25000000 | tf_op jit(solution)/shard_map/pallas_call | solution.py:529
  65.4 2.3 %copy.11 = bf16[512,1024]{1,0:T(8,128)(2,1)} copy(bf16[512,1024]{1,0:T(8,128)(2,1)} %shard_map.91) | data formatting | bytes 2097152
